TPU v7x, 256 devices: a whole 4x4x8 slice. The times are simulated.
256 devices in a mesh: frames: 32 (over z, x), heads: 8 (over y, core).
Axes of the slice: x: 4, y: 4, z: 8, core: 2. Of those that a mesh axis runs over, the one named last changes fastest.
Arguments:
- frames: bfloat16 [32768, 1024], P('frames', 'heads'), may hold values from -6 to 6
- latents: bfloat16 [512, 1024], replicated, may hold values from -6 to 6
- cross_query: bfloat16 [2, 1024, 1024], P(None, None, 'heads'), may hold values from -0.1875 to 0.1875
- cross_key: bfloat16 [2, 1024, 1024], P(None, None, 'heads'), may hold values from -0.1875 to 0.1875
- cross_value: bfloat16 [2, 1024, 1024], P(None, None, 'heads'), may hold values from -0.1875 to 0.1875
- cross_out: bfloat16 [2, 1024, 1024], P(None, 'heads'), may hold values from -0.1875 to 0.1875
- self_query: bfloat16 [2, 1024, 1024], P(None, None, 'heads'), may hold values from -0.1875 to 0.1875
- self_key: bfloat16 [2, 1024, 1024], P(None, None, 'heads'), may hold values from -0.1875 to 0.1875
- self_value: bfloat16 [2, 1024, 1024], P(None, None, 'heads'), may hold values from -0.1875 to 0.1875
- self_out: bfloat16 [2, 1024, 1024], P(None, 'heads'), may hold values from -0.1875 to 0.1875
- mlp_in: bfloat16 [2, 1024, 4096], P(None, None, 'heads'), may hold values from -0.1875 to 0.1875
- mlp_out: bfloat16 [2, 4096, 1024], P(None, 'heads'), may hold values from -0.09375 to 0.09375
Outputs:
- encoded: float32 [512, 1024], P('frames')
- midway: float32 [512, 1024], P(None, 'heads')
All inputs are finite; a program needn't handle non-finite values.
Results may differ from a plain program's by a relative error of at most 0.007.
Values may be sent and summed in bfloat16 or wider, within the bound.
A program may use at most 64 MiB of HBM per device.

v0:
```python
import jax
import jax.numpy as jnp
from jax import lax
from jax.sharding import Mesh
from jax.sharding import PartitionSpec as P

D = 1024
HEAD_DIM = 64
PASSES = 2
FRAMES = ("frames_0", "frames_1")


epsilon = 1e-05


def sent_to_all(value, axis):
    peers = lax.axis_size(axis)
    return lax.all_to_all(
        jnp.broadcast_to(value[None], (peers, *value.shape)), axis, 0, 0, tiled=True
    )


def taken_together(value, axis):
    everything = sent_to_all(value, axis)
    return jnp.max(everything, axis=0)


def split_up(value, dim, peers):
    before, after = (value.shape[:dim], value.shape[dim + 1 :])
    return jnp.moveaxis(value.reshape(*before, peers, -1, *after), dim, 0)


def sum_at_owner(value, axis, dim):
    peers = lax.axis_size(axis)
    parts = lax.all_to_all(split_up(value, dim, peers), axis, 0, 0, tiled=True)
    return jnp.sum(parts, axis=0)


def in_one_piece(arrays, axis, dim, along):
    both = jnp.concatenate(arrays, axis=along)
    out, at, done = (sum_at_owner(both, axis, dim), 0, [])
    for a in arrays:
        done.append(lax.slice_in_dim(out, at, at + a.shape[along], axis=along))
        at += a.shape[along]
    return tuple(done)


def of_everyone(value, axis):
    everything = sent_to_all(value, axis)
    return jnp.sum(everything, axis=0)


def in_order(parts, dim):
    parts = jnp.moveaxis(parts, 0, dim)
    lengths = parts.shape
    return parts.reshape(*lengths[:dim], lengths[dim] * lengths[dim + 1], *lengths[dim + 2 :])


def gather_directly(value, axis, dim):
    return in_order(sent_to_all(value, axis), dim)


def gathered_by_axis(value, axes, dim):
    if not axes:
        return value
    nearer = lax.all_gather(value, axes[-1], axis=dim, tiled=True)
    return gathered_by_axis(nearer, axes[:-1], dim)


def layer_norm(vector):
    centre = vector - jnp.mean(vector, axis=-1, keepdims=True)
    spread_sq = jnp.mean(centre * centre, axis=-1, keepdims=True)
    return centre * lax.rsqrt(spread_sq + epsilon)


def project(left_side, weight):
    return jnp.dot(left_side, weight, preferred_element_type=jnp.float32)


def spread(per_head):
    return jnp.repeat(per_head, HEAD_DIM, axis=1)


def cross_context(queries, key_rows, value_rows):
    latent_count, columns = queries.shape
    frame_count = key_rows.shape[0]
    local_heads = columns // HEAD_DIM
    query_heads = queries.reshape(latent_count, local_heads, HEAD_DIM)
    key_heads = key_rows.reshape(frame_count, local_heads, HEAD_DIM)
    value_heads = value_rows.reshape(frame_count, local_heads, HEAD_DIM).astype(jnp.float32)
    scores = jnp.einsum("lhd,fhd->lhf", query_heads, key_heads, preferred_element_type=jnp.float32)
    highest = jnp.max(scores, axis=2)
    exponent_terms = jnp.exp(scores - highest[:, :, None])
    totals = jnp.sum(exponent_terms, axis=2)
    weighted = jnp.einsum(
        "lhf,fhd->lhd", exponent_terms, value_heads, precision=lax.Precision.HIGHEST
    )
    weighted = weighted.reshape(latent_count, columns)
    overall = taken_together(highest, FRAMES)
    factor = jnp.exp(highest - overall)
    totals, weighted = in_one_piece((totals * factor, weighted * spread(factor)), FRAMES, 0, 1)
    return (weighted / spread(totals)).astype(jnp.bfloat16)


def self_context(queries, key_rows, value_rows):
    query_count, columns = queries.shape
    latent_count = key_rows.shape[0]
    local_heads = columns // HEAD_DIM
    query_heads = queries.reshape(query_count, local_heads, HEAD_DIM)
    key_heads = key_rows.reshape(latent_count, local_heads, HEAD_DIM)
    value_heads = value_rows.reshape(latent_count, local_heads, HEAD_DIM)
    scores = jnp.einsum("ihd,khd->hik", query_heads, key_heads, preferred_element_type=jnp.float32)
    weights = jax.nn.softmax(scores, axis=-1).astype(jnp.bfloat16)
    context = jnp.einsum("hik,khd->ihd", weights, value_heads, preferred_element_type=jnp.float32)
    return context.reshape(query_count, columns).astype(jnp.bfloat16)


def head_total(partial_value):
    return of_everyone(partial_value, "heads")


def column_share(latent_state):
    column_count = D // lax.axis_size("heads")
    column_start = lax.axis_index("heads") * column_count
    return lax.dynamic_slice_in_dim(latent_state, column_start, column_count, 1)


def local(
    frames,
    latents,
    cross_query,
    cross_key,
    cross_value,
    cross_out,
    self_query,
    self_key,
    self_value,
    self_out,
    mlp_in,
    mlp_out,
):
    score_scale = 1.0 / HEAD_DIM**0.5
    gathered = gather_directly(frames, "heads", 1)
    normed = layer_norm(gathered.astype(jnp.float32)).astype(jnp.bfloat16)
    latent_state = latents.astype(jnp.float32)
    latent_count = latents.shape[0]
    row_count = latent_count // lax.axis_size(FRAMES)
    row_start = lax.axis_index(FRAMES) * row_count
    own_rows = lax.dynamic_slice_in_dim(latent_state, row_start, row_count, 0)
    midway = column_share(latent_state)
    for pass_index in range(PASSES):
        cross_in = layer_norm(latent_state).astype(jnp.bfloat16)
        queries = (project(cross_in, cross_query[pass_index]) * score_scale).astype(jnp.bfloat16)
        key_rows = project(normed, cross_key[pass_index]).astype(jnp.bfloat16)
        value_rows = project(normed, cross_value[pass_index]).astype(jnp.bfloat16)
        context = cross_context(queries, key_rows, value_rows)
        context_rows = context
        own_rows = own_rows + head_total(project(context_rows, cross_out[pass_index]))
        latent_state = gathered_by_axis(own_rows, FRAMES, 0)
        self_in = layer_norm(latent_state).astype(jnp.bfloat16)
        self_rows = lax.dynamic_slice_in_dim(self_in, row_start, row_count, 0)
        self_q = (project(self_rows, self_query[pass_index]) * score_scale).astype(jnp.bfloat16)
        self_k = project(self_in, self_key[pass_index]).astype(jnp.bfloat16)
        self_v = project(self_in, self_value[pass_index]).astype(jnp.bfloat16)
        context = self_context(self_q, self_k, self_v)
        own_rows = own_rows + head_total(project(context, self_out[pass_index]))
        mlp_norm = layer_norm(own_rows).astype(jnp.bfloat16)
        hidden = jax.nn.gelu(project(mlp_norm, mlp_in[pass_index]), approximate=False).astype(
            jnp.bfloat16
        )
        own_rows = own_rows + head_total(project(hidden, mlp_out[pass_index]))
        if pass_index + 1 < PASSES:
            latent_state = gathered_by_axis(own_rows, FRAMES, 0)
        if pass_index == 0:
            midway = column_share(latent_state)
    return (own_rows, midway)


def solution(mesh):
    torus = Mesh(mesh.devices.reshape(8, 4, mesh.shape["heads"]), ("frames_0", "frames_1", "heads"))
    placed = (
        P(FRAMES, "heads"),
        P(),
        P(None, None, "heads"),
        P(None, None, "heads"),
        P(None, None, "heads"),
        P(None, "heads", None),
        P(None, None, "heads"),
        P(None, None, "heads"),
        P(None, None, "heads"),
        P(None, "heads", None),
        P(None, None, "heads"),
        P(None, "heads", None),
    )
    return jax.shard_map(
        local,
        mesh=torus,
        in_specs=placed,
        out_specs=(P(FRAMES, None), P(None, "heads")),
        check_vma=False,
    )
```

profile of v0, /device:TPU:1, one launch (start us, length us, event | category | flops | bytes accessed | tf_op | source)
XLA Modules:
  0.0 406.4 jit_solution(5271510928416912543)
XLA Ops:
  7.2 1.1 copy.44
  8.3 1.6 broadcast_in_dim.26
  9.9 6.9 %all-to-all-start = ((bf16[8,1024,128]{1,2,0:T(8,128)(2,1)}), bf16[8,1024,128]{1,2,0:T(8,128)(2,1)S(1)}, u32[]{:S(2)}, u32[]{:S(2)}) async-start(bf16[8,1024,128]{1,2,0:T(8,128)(2,1)} %broadcast_in_dim.26), calls=%async_computation | async-start | bytes 4194304 | tf_op jit(solution)/shard_map/all_to_all | solution.py:18
  17.0 0.4 multiply_reduce_fusion.3
  17.4 0.4 copy-done.16
  17.8 0.6 fusion.28
  18.4 24.7 %all-to-all-done = bf16[8,1024,128]{1,2,0:T(8,128)(2,1)S(1)} async-done(((bf16[8,1024,128]{1,2,0:T(8,128)(2,1)}), bf16[8,1024,128]{1,2,0:T(8,128)(2,1)S(1)}, u32[]{:S(2)}, u32[]{:S(2)}) %all-to-all-start) | async-done | bytes 2097184 | tf_op jit(solution)/shard_map/all_to_all | solution.py:18
  43.5 0.6 fusion.4
  44.1 0.6 fusion.5
  44.7 0.4 copy-done.18
  45.1 0.5 convolution_convert_fusion.3
  46.0 0.8 bitcast_reduce_fusion.1
  46.8 0.6 fusion.10
  47.4 1.5 copy-done
  48.9 0.7 broadcast_in_dim.27
  49.6 10.2 %all-to-all-start.1 = ((f32[32,512,2]{1,2,0:T(2,128)}), f32[32,512,2]{1,2,0:T(2,128)S(1)}, u32[]{:S(2)}, u32[]{:S(2)}) async-start(f32[32,512,2]{1,2,0:T(2,128)} %broadcast_in_dim.27), calls=%async_computation.1 | async-start | bytes 262144 | tf_op jit(solution)/shard_map/all_to_all | solution.py:18
  59.9 1.4 convolution_convert_fusion.2
  61.3 7.9 %all-to-all-done.1 = f32[32,512,2]{1,2,0:T(2,128)S(1)} async-done(((f32[32,512,2]{1,2,0:T(2,128)}), f32[32,512,2]{1,2,0:T(2,128)S(1)}, u32[]{:S(2)}, u32[]{:S(2)}) %all-to-all-start.1) | async-done | bytes 131104 | tf_op jit(solution)/shard_map/all_to_all | solution.py:18
  69.3 4.2 %fusion.25 = f32[512,2,64]{0,2,1:T(8,128)S(1)} fusion(bf16[1024,2,64]{0,2,1:T(8,128)(2,1)S(1)} %bitcast.153, f32[2,1024,512]{2,1,0:T(8,128)} %copy-done, f32[512,2]{0,1:T(2,128)S(1)} %get-tuple-element.10, f32[512,2]{0,1:T(2,128)S(1)} %get-tuple-element.9), kind=kOutput, calls=%fused_computation.36 | convolution fusion | flops 806420480 | bytes 4726784 | tf_op jit(solution)/shard_map/lhf,fhd->lhd/dot_general | solution.py:95
  74.5 17.9 %all_to_all.55 = f32[32,16,130]{2,1,0:T(8,128)S(1)} all-to-all(f32[32,16,130]{2,1,0:T(8,128)S(1)} %pad_maximum_fusion), channel_id=1, replica_groups=mesh['frames_0'=8,'frames_1'=4,'heads'=8] {'frames_0','frames_1'}, dimensions={0} | all-to-all | bytes 532480 | tf_op jit(solution)/shard_map/all_to_all | solution.py:35
  92.7 0.9 broadcast_in_dim.30
  93.6 8.3 %all-to-all-start.3 = ((f32[8,16,1024]{2,1,0:T(8,128)}), f32[8,16,1024]{2,1,0:T(8,128)}, u32[]{:S(2)}, u32[]{:S(2)}) async-start(f32[8,16,1024]{2,1,0:T(8,128)} %broadcast_in_dim.30), calls=%async_computation.3 | async-start | bytes 1048576 | tf_op jit(solution)/shard_map/all_to_all | solution.py:18
  102.2 9.4 %all-to-all-done.3 = f32[8,16,1024]{2,1,0:T(8,128)} async-done(((f32[8,16,1024]{2,1,0:T(8,128)}), f32[8,16,1024]{2,1,0:T(8,128)}, u32[]{:S(2)}, u32[]{:S(2)}) %all-to-all-start.3) | async-done | bytes 524320 | tf_op jit(solution)/shard_map/all_to_all | solution.py:18
  111.5 1.1 reduce_sum.240
  112.6 10.4 %all_gather.18 = f32[64,1024]{1,0:T(8,128)} all-gather(f32[16,1024]{1,0:T(8,128)S(1)} %dynamic-slice_add_fusion), channel_id=1, replica_groups=mesh['frames_0'=8,'frames_1'=4,'heads'=8] {'frames_1'}, dimensions={0}, use_global_device_ids=true | all-gather | bytes 327680 | tf_op jit(solution)/shard_map/all_gather | solution.py:66
  123.1 34.4 %all-gather.4.cloned.1.call-done = f32[512,1024]{1,0:T(8,128)} async-done(((f32[64,1024]{1,0:T(8,128)}), f32[512,1024]{1,0:T(8,128)}) %all-gather.4.cloned.1.call-update) | async-done | bytes 2097168 | tf_op jit(solution)/shard_map/all_gather | solution.py:66
  157.5 1.9 reduce_sum.241
  160.4 0.7 copy-done.12
  161.1 0.5 convolution_convert_fusion.7
  161.6 0.5 convolution_convert_fusion.6
  163.3 17.8 %all_to_all.56 = f32[8,16,1024]{2,1,0:T(8,128)S(1)} all-to-all(f32[8,16,1024]{2,1,0:T(8,128)S(1)} %broadcast_in_dim.31), channel_id=1, replica_groups=mesh['frames_0'=8,'frames_1'=4,'heads'=8] {'heads'}, dimensions={0} | all-to-all | bytes 1048576 | tf_op jit(solution)/shard_map/all_to_all | solution.py:18
  181.5 2.1 fusion.42
  183.7 13.1 %all_to_all.57 = f32[8,16,1024]{2,1,0:T(8,128)S(1)} all-to-all(f32[8,16,1024]{2,1,0:T(8,128)S(1)} %broadcast_in_dim.32), channel_id=1, replica_groups=mesh['frames_0'=8,'frames_1'=4,'heads'=8] {'heads'}, dimensions={0} | all-to-all | bytes 1048576 | tf_op jit(solution)/shard_map/all_to_all | solution.py:18
  196.8 10.9 %all_gather.20 = f32[64,1024]{1,0:T(8,128)} all-gather(f32[16,1024]{1,0:T(8,128)S(1)} %add.97), channel_id=1, replica_groups=mesh['frames_0'=8,'frames_1'=4,'heads'=8] {'frames_1'}, dimensions={0}, use_global_device_ids=true | all-gather | bytes 327680 | tf_op jit(solution)/shard_map/all_gather | solution.py:66
  207.8 1.5 convolution_convert_fusion
  209.3 0.5 convolution_convert_fusion.1
  209.8 34.4 %all-gather.6.cloned.1.call-done = f32[512,1024]{1,0:T(8,128)} async-done(((f32[64,1024]{1,0:T(8,128)}), f32[512,1024]{1,0:T(8,128)}) %all-gather.6.cloned.1.call-update) | async-done | bytes 2097168 | tf_op jit(solution)/shard_map/all_gather | solution.py:66
  244.2 1.9 reduce_sum.248
  246.8 0.5 copy-done.17
  247.3 0.6 fusion.29
  247.9 2.7 bitcast_reduce_fusion
  250.6 0.7 broadcast_in_dim.33
  251.3 6.8 %all-to-all-start.6 = ((f32[32,512,2]{1,2,0:T(2,128)}), f32[32,512,2]{1,2,0:T(2,128)S(1)}, u32[]{:S(2)}, u32[]{:S(2)}) async-start(f32[32,512,2]{1,2,0:T(2,128)} %broadcast_in_dim.33), calls=%async_computation.6 | async-start | bytes 262144 | tf_op jit(solution)/shard_map/all_to_all | solution.py:18
  258.2 2.8 fusion.13
  260.9 6.5 %all-to-all-done.6 = f32[32,512,2]{1,2,0:T(2,128)S(1)} async-done(((f32[32,512,2]{1,2,0:T(2,128)}), f32[32,512,2]{1,2,0:T(2,128)S(1)}, u32[]{:S(2)}, u32[]{:S(2)}) %all-to-all-start.6) | async-done | bytes 131104 | tf_op jit(solution)/shard_map/all_to_all | solution.py:18
  267.5 4.2 %fusion.19 = f32[512,2,64]{0,2,1:T(8,128)S(1)} fusion(bf16[1024,2,64]{0,2,1:T(8,128)(2,1)S(1)} %bitcast.152, f32[2,1024,512]{2,1,0:T(8,128)} %get-tuple-element.13, f32[512,2]{0,1:T(2,128)S(1)} %get-tuple-element.12, f32[512,2]{0,1:T(2,128)S(1)} %get-tuple-element.5), kind=kOutput, calls=%fused_computation.34 | convolution fusion | flops 806420480 | bytes 4726784 | tf_op jit(solution)/shard_map/lhf,fhd->lhd/dot_general | solution.py:95
  272.7 15.8 %all_to_all.58 = f32[32,16,130]{2,1,0:T(8,128)S(1)} all-to-all(f32[32,16,130]{2,1,0:T(8,128)S(1)} %pad_maximum_fusion.1), channel_id=1, replica_groups=mesh['frames_0'=8,'frames_1'=4,'heads'=8] {'frames_0','frames_1'}, dimensions={0} | all-to-all | bytes 532480 | tf_op jit(solution)/shard_map/all_to_all | solution.py:35
  288.7 1.2 fusion.59
  289.9 20.5 %all_to_all.59 = f32[8,16,1024]{2,1,0:T(8,128)S(1)} all-to-all(f32[8,16,1024]{2,1,0:T(8,128)S(1)} %broadcast_in_dim.36), channel_id=1, replica_groups=mesh['frames_0'=8,'frames_1'=4,'heads'=8] {'heads'}, dimensions={0} | all-to-all | bytes 1048576 | tf_op jit(solution)/shard_map/all_to_all | solution.py:18
  310.5 10.5 %all_gather.22 = f32[64,1024]{1,0:T(8,128)} all-gather(f32[16,1024]{1,0:T(8,128)S(1)} %add.99), channel_id=1, replica_groups=mesh['frames_0'=8,'frames_1'=4,'heads'=8] {'frames_1'}, dimensions={0}, use_global_device_ids=true | all-gather | bytes 327680 | tf_op jit(solution)/shard_map/all_gather | solution.py:66
  321.0 34.6 %all-gather.8.cloned.1.call-done = f32[512,1024]{1,0:T(8,128)} async-done(((f32[64,1024]{1,0:T(8,128)}), f32[512,1024]{1,0:T(8,128)}) %all-gather.8.cloned.1.call-update) | async-done | bytes 2097168 | tf_op jit(solution)/shard_map/all_gather | solution.py:66
  355.6 1.8 reduce_sum.253
  357.3 2.1 multiply_reduce_fusion
  359.8 0.7 copy-done.13
  360.5 1.1 convolution_convert_fusion.5
  361.6 0.5 convolution_convert_fusion.4
  362.7 1.1 fusion.35
  364.1 17.8 %all_to_all.60 = f32[8,16,1024]{2,1,0:T(8,128)S(1)} all-to-all(f32[8,16,1024]{2,1,0:T(8,128)S(1)} %broadcast_in_dim.37), channel_id=1, replica_groups=mesh['frames_0'=8,'frames_1'=4,'heads'=8] {'heads'}, dimensions={0} | all-to-all | bytes 1048576 | tf_op jit(solution)/shard_map/all_to_all | solution.py:18
  382.3 2.1 fusion.38
  384.5 0.8 broadcast_in_dim.38
  385.3 4.4 %all-to-all-start.10 = ((f32[8,16,1024]{2,1,0:T(8,128)}), f32[8,16,1024]{2,1,0:T(8,128)S(1)}, u32[]{:S(2)}, u32[]{:S(2)}) async-start(f32[8,16,1024]{2,1,0:T(8,128)} %broadcast_in_dim.38), calls=%async_computation.10 | async-start | bytes 1048576 | tf_op jit(solution)/shard_map/all_to_all | solution.py:18
  389.7 0.7 constant_dynamic-slice_fusion
  390.5 8.8 %all-to-all-done.10 = f32[8,16,1024]{2,1,0:T(8,128)S(1)} async-done(((f32[8,16,1024]{2,1,0:T(8,128)}), f32[8,16,1024]{2,1,0:T(8,128)S(1)}, u32[]{:S(2)}, u32[]{:S(2)}) %all-to-all-start.10) | async-done | bytes 524320 | tf_op jit(solution)/shard_map/all_to_all | solution.py:18
  399.3 0.6 add.103
  (113 shorter events, 8.9 us)
Async XLA Ops:
  9.9 6.9 %copy-start.4 = (bf16[512,1024]{1,0:T(8,128)(2,1)S(1)}, bf16[512,1024]{1,0:T(8,128)(2,1)}, u32[]{:S(2)}) copy-start(bf16[512,1024]{1,0:T(8,128)(2,1)} %param.13) | copy-start | bytes 3145732
  9.9 33.2 %all-to-all-start = ((bf16[8,1024,128]{1,2,0:T(8,128)(2,1)}), bf16[8,1024,128]{1,2,0:T(8,128)(2,1)S(1)}, u32[]{:S(2)}, u32[]{:S(2)}) async-start(bf16[8,1024,128]{1,2,0:T(8,128)(2,1)} %broadcast_in_dim.26), calls=%async_computation | async-start | bytes 4194304 | tf_op jit(solution)/shard_map/all_to_all | solution.py:18
  16.8 1.0 copy-start.16
  44.1 1.0 copy-start.18
  44.7 1.3 copy-start.5
  46.8 2.1 copy-start
  46.8 13.1 %copy-start.6 = (bf16[8,1024,128]{1,2,0:T(8,128)(2,1)S(1)}, bf16[8,1024,128]{1,2,0:T(8,128)(2,1)}, u32[]{:S(2)}) copy-start(bf16[8,1024,128]{1,2,0:T(8,128)(2,1)} %copy-done.5) | copy-start | bytes 6291460
  49.6 19.6 %all-to-all-start.1 = ((f32[32,512,2]{1,2,0:T(2,128)}), f32[32,512,2]{1,2,0:T(2,128)S(1)}, u32[]{:S(2)}, u32[]{:S(2)}) async-start(f32[32,512,2]{1,2,0:T(2,128)} %broadcast_in_dim.27), calls=%async_computation.1 | async-start | bytes 262144 | tf_op jit(solution)/shard_map/all_to_all | solution.py:18
  73.5 19.0 %copy-start.9 = (bf16[2,128,1024]{2,1,0:T(8,128)(2,1)S(1)}, bf16[2,128,1024]{2,1,0:T(8,128)(2,1)}, u32[]{:S(2)}) copy-start(bf16[2,128,1024]{2,1,0:T(8,128)(2,1)} %param.17) | copy-start | bytes 1572868
  93.6 17.9 %all-to-all-start.3 = ((f32[8,16,1024]{2,1,0:T(8,128)}), f32[8,16,1024]{2,1,0:T(8,128)}, u32[]{:S(2)}, u32[]{:S(2)}) async-start(f32[8,16,1024]{2,1,0:T(8,128)} %broadcast_in_dim.30), calls=%async_computation.3 | async-start | bytes 1048576 | tf_op jit(solution)/shard_map/all_to_all | solution.py:18
  101.9 55.5 %all-gather.4.cloned.1.call-start = ((), (), s32[]{:S(2)}) async-start(), calls=%async_computation.11 | async-start | bytes 2359296 | tf_op jit(solution)/shard_map/all_gather | solution.py:66
  123.1 121.2 %all-gather.6.cloned.1.call-start = ((), (), s32[]{:S(2)}) async-start(), calls=%async_computation.12 | async-start | bytes 2359296 | tf_op jit(solution)/shard_map/all_gather | solution.py:66
  157.5 2.2 copy-start.2
  160.0 1.0 copy-start.12
  160.1 1.5 copy-start.14
  161.1 1.1 copy-start.8
  161.1 2.0 copy-start.10
  183.6 24.1 %copy-start.7 = (bf16[8,1024,128]{1,2,0:T(8,128)(2,1)S(1)}, bf16[8,1024,128]{1,2,0:T(8,128)(2,1)}, u32[]{:S(2)}) copy-start(bf16[8,1024,128]{1,2,0:T(8,128)(2,1)} %copy-done.5) | copy-start | bytes 6291460
  207.7 1.5 copy-start.19
  244.2 2.2 copy-start.1
  246.1 1.1 copy-start.17
  251.3 16.2 %all-to-all-start.6 = ((f32[32,512,2]{1,2,0:T(2,128)}), f32[32,512,2]{1,2,0:T(2,128)S(1)}, u32[]{:S(2)}, u32[]{:S(2)}) async-start(f32[32,512,2]{1,2,0:T(2,128)} %broadcast_in_dim.33), calls=%async_computation.6 | async-start | bytes 262144 | tf_op jit(solution)/shard_map/all_to_all | solution.py:18
  258.1 97.4 %all-gather.8.cloned.1.call-start = ((), (), s32[]{:S(2)}) async-start(), calls=%async_computation.13 | async-start | bytes 2359296 | tf_op jit(solution)/shard_map/all_gather | solution.py:66
  357.3 2.2 copy-start.3
  359.4 1.1 copy-start.13
  359.5 2.1 copy-start.15
  360.5 3.4 copy-start.11
  385.3 13.9 %all-to-all-start.10 = ((f32[8,16,1024]{2,1,0:T(8,128)}), f32[8,16,1024]{2,1,0:T(8,128)S(1)}, u32[]{:S(2)}, u32[]{:S(2)}) async-start(f32[8,16,1024]{2,1,0:T(8,128)} %broadcast_in_dim.38), calls=%async_computation.10 | async-start | bytes 1048576 | tf_op jit(solution)/shard_map/all_to_all | solution.py:18
Sparse Core Ops, SparseCore 0:
  123.2 34.2 all-gather.3
  207.9 36.3 all-gather.5
  321.1 34.4 all-gather.7
where the time goes:
time: 408 us; the launch traced here: 406 us
  waiting for transfers between devices  161 us (39%)
  blocking collectives  135 us (33%)
  starting transfers between devices  36.8 us (9%)
  matrix products  27.5 us (7%)
  other arithmetic  18.3 us (4%)
  local copies, waits for them, and re-layouts  14.2 us (3%)
  between operations  14.2 us (3%)
    all_gather x3, waiting for transfers between devices, gathered_by_axis(): nearer = lax.all_gather(value, axes[-1], axis=dim, tiled=True)  103 us
    all_to_all x4, blocking collectives, sent_to_all(): lax.all_to_all(jnp.broadcast_to(value[None], (peers, *value.shape)), axis...  69.3 us
    all_to_all x5, waiting for transfers between devices, sent_to_all(): lax.all_to_all(jnp.broadcast_to(value[None], (peers, *value.shape)), axis...  57.2 us
    all_to_all x5, starting transfers between devices, sent_to_all(): lax.all_to_all(jnp.broadcast_to(value[None], (peers, *value.shape)), axis...  36.7 us
    all_to_all x2, blocking collectives, sum_at_owner(): parts = lax.all_to_all(split_up(value, dim, peers), axis, 0, 0, tiled=True)  33.7 us
    all_gather x3, blocking collectives, gathered_by_axis(): nearer = lax.all_gather(value, axes[-1], axis=dim, tiled=True)  31.7 us
    dot_general x18, matrix products, project(): return jnp.dot(left_side, weight, preferred_element_type=jnp.float32)  14 us
    dot_general x2, matrix products, cross_context(): jnp.einsum('lhf,fhd->lhd', exponent_terms, value_heads, precision=lax.Pre...  8.47 us
  transfers between devices with their start and end apart: 8, of which 8 were waited for; matrix products, arithmetic and copies ran while one was open for 2% of the time, Pallas kernels for 0%

commit v1 on v0

v1 whole, which is shorter than its diff:
```python
import functools

import jax
import jax.numpy as jnp
from jax import lax
from jax.experimental import pallas as pl
from jax.experimental.pallas import tpu as pltpu
from jax.sharding import PartitionSpec as P

EPSILON = 1e-05
HEAD_DIM = 64
MESH = pl.DeviceIdType.MESH
F32 = jnp.float32
BF16 = jnp.bfloat16
CHUNKS = 4
LANES = 128
ONES = 16
PART, STAT, CROSS, KEYS, SELF, MLP, QUERY, MID = range(8)


def layer_norm(v):
    centre = v - jnp.mean(v, axis=-1, keepdims=True)
    spread = jnp.mean(centre * centre, axis=-1, keepdims=True)
    return centre * lax.rsqrt(spread + EPSILON)


def project(a, b):
    return jnp.dot(a, b, preferred_element_type=F32)


def against(a, b):
    return lax.dot_general(a, b, (((1,), (1,)), ((), ())), preferred_element_type=F32)


def lane(shape):
    return lax.broadcasted_iota(jnp.int32, shape, len(shape) - 1)


def by_head(q):
    first = lane(q.shape) < HEAD_DIM
    zero = jnp.zeros_like(q)
    return jnp.concatenate([jnp.where(first, q, zero), jnp.where(first, zero, q)], axis=0)


def kernel(
    nf, nh,
    frames, latents, cq, ck, cv, co, sq, sk, sv, so, mi, mo,
    encoded, midway,
    x_s, lat_s, cq_s, ckv_s, co_s, sqkv_s, so_s, mi_s, mo_s,
    k_s, vt_s, qall_s, m_s, acc_s, o_s, st_s, po_s, ps_s, tr_s, kv_s, sum_s, row_s, mid_s,
    w_sem, own_sem, ring_recv, ring_send, recv_sem, send_sem,
):
    f, h = lax.axis_index("frames"), lax.axis_index("heads")
    latent_count, width = lat_s.shape
    frame_count = x_s.shape[0]
    rows_each = latent_count // nf
    chunk = frame_count // CHUNKS
    half = chunk // 2
    passes = cq_s.shape[0]

    sib = h + 1 - 2 * lax.rem(h, 2)
    right, left, opp = lax.rem(h + 2, nh), lax.rem(h + nh - 2, nh), lax.rem(h + 4, nh)

    def cols(who):
        return pl.ds(pl.multiple_of(who * LANES, LANES), LANES)

    own_rows = pl.ds(pl.multiple_of(f * rows_each, rows_each), rows_each)

    def local_copies():
        groups = [
            [(latents, lat_s)],
            [(cq, cq_s)],
            [(w.at[p], ckv_s.at[:, pl.ds((2 * p + i) * LANES, LANES)]) for p in range(passes) for i, w in enumerate((ck, cv))],
            [(co, co_s)],
            [(w, sqkv_s.at[:, :, pl.ds(i * LANES, LANES)]) for i, w in enumerate((sq, sk, sv))],
            [(so, so_s)],
            [(mi, mi_s)],
            [(mo, mo_s)],
        ]
        return groups

    for k in range(CHUNKS):
        r = pl.ds(k * chunk, chunk)
        pltpu.make_async_copy(frames.at[r, :], x_s.at[r, cols(h)], own_sem.at[k]).start()
    for i, group in enumerate(local_copies()):
        for src, dst in group:
            pltpu.make_async_copy(src, dst, w_sem.at[i]).start()

    def loaded(i, ref):
        pltpu.make_async_copy(ref, ref, w_sem.at[i]).wait()

    barrier = pltpu.get_barrier_semaphore()

    def greet_f(p, _):
        pl.semaphore_signal(barrier, inc=1, device_id=(lax.rem(f + p, nf), h), device_id_type=MESH)
        return 0

    def greet_h(p, _):
        pl.semaphore_signal(barrier, inc=1, device_id=(f, lax.rem(h + p, nh)), device_id_type=MESH)
        return 0

    lax.fori_loop(1, nh, greet_h, 0)
    lax.fori_loop(1, nf, greet_f, 0)
    pl.semaphore_wait(barrier, nf + nh - 2)

    L, R, OA, OB, S_OWN, S_L, S_R, S_OA, S_OB = range(9)

    def ring(kind, k, src, dst, to):
        return pltpu.make_async_remote_copy(
            src, dst, ring_send, ring_recv.at[kind, k], device_id=(f, to), device_id_type=MESH
        )

    def block(k, who, part=None):
        start, size = (k * chunk, chunk) if part is None else (k * chunk + part * half, half)
        return x_s.at[pl.ds(pl.multiple_of(start, half), size), cols(who)]

    def arrived(kind, k, ref):
        ring(kind, k, ref, ref, sib).wait_recv()

    def send_own(k, _):
        src = frames.at[pl.ds(pl.multiple_of(k * chunk, chunk), chunk), :]
        ring(L, k, src, block(k, h), right).start()
        ring(R, k, src, block(k, h), left).start()
        ring(S_OWN, k, src, block(k, h), sib).start()
        return 0

    lax.fori_loop(0, CHUNKS, send_own, 0)

    def set_queries(p, q):
        qall_s[p] = q

    loaded(0, lat_s)
    loaded(1, cq_s)
    state = lat_s[...].astype(F32)
    q0 = (project(layer_norm(state).astype(BF16), cq_s[0]) * 0.125).astype(BF16)
    set_queries(0, q0)
    rows = lat_s[own_rows, :].astype(F32)
    for p in range(passes):
        vt_s[p, pl.ds(LANES, ONES), :] = jnp.ones((ONES, frame_count), BF16)
    loaded(2, ckv_s)

    def keys_values(k):
        r = pl.ds(pl.multiple_of(k * chunk, chunk), chunk)
        normed = layer_norm(x_s[r, :].astype(F32)).astype(BF16)
        both = project(normed, ckv_s[...])
        for p in range(passes):
            k_s[p, r, :] = both[:, 2 * p * LANES:(2 * p + 1) * LANES].astype(BF16)
            value = both[:, (2 * p + 1) * LANES:(2 * p + 2) * LANES]
            vt_s[p, pl.ds(0, LANES), r] = value.T.astype(BF16)

    def attend_start():
        m_s[...] = jnp.full_like(m_s, -jnp.inf)
        acc_s[...] = jnp.zeros_like(acc_s)

    def attend(p, k):
        r = pl.ds(pl.multiple_of(k * chunk, chunk), chunk)
        scores = against(k_s[p, r, :], by_head(qall_s[p]))
        before = m_s[...]
        highest = jnp.maximum(before, jnp.max(scores, axis=0, keepdims=True))
        terms = jnp.exp(scores - highest).astype(BF16)
        acc_s[...] = acc_s[...] * jnp.exp(before - highest) + project(vt_s[p, :, r], terms)
        m_s[...] = highest

    def exchange_f(kind, p, pairs):
        def send(d, _):
            t = lax.rem(f + d, nf)
            for i, (src_of, dst, _all) in enumerate(pairs):
                pltpu.make_async_remote_copy(
                    src_of(t), dst, send_sem.at[p, kind + i], recv_sem.at[p, kind + i],
                    device_id=(t, h), device_id_type=MESH,
                ).start()
            return 0
        lax.fori_loop(1, nf, send, 0)

    def landed(kind, p, ref):
        pltpu.make_async_remote_copy(
            ref, ref, send_sem.at[p, kind], recv_sem.at[p, kind], device_id=(f, sib), device_id_type=MESH
        ).wait_recv()

    def sent(kind, p, ref):
        pltpu.make_async_remote_copy(
            ref, ref, send_sem.at[p, kind], recv_sem.at[p, kind], device_id=(f, sib), device_id_type=MESH
        ).wait_send()

    def attend_end(p):
        total = acc_s[pl.ds(LANES, 1), :]
        value = acc_s[pl.ds(0, LANES), :] / total
        both = jnp.concatenate(
            [value[:HEAD_DIM, :latent_count], value[HEAD_DIM:, latent_count:]], axis=0
        )
        o_s[p] = both.T.astype(BF16)
        level = m_s[...] + jnp.log(total)
        for t in range(latent_count // LANES):
            for i in range(2):
                at = i * latent_count + t * LANES
                st_s[p, t, pl.ds(i, 1), :] = level[:, at:at + LANES]

        def rows_of(t):
            return pl.ds(pl.multiple_of(t * rows_each, rows_each), rows_each)

        per_tile = LANES // rows_each
        exchange_f(PART, p, [
            (lambda t: o_s.at[p, rows_of(t), :], po_s.at[p, f], None),
            (lambda t: st_s.at[p, t // per_tile], ps_s.at[p, f], None),
        ])
        po_s[p, f] = o_s[p, own_rows, :]
        ps_s[p, f] = st_s[p, f // per_tile]
        landed(STAT, p, ps_s.at[p, pl.ds(0, nf - 1)])
        levels = jnp.concatenate([ps_s[p, :, 0, :], ps_s[p, :, 1, :]], axis=0)
        tr_s[...] = levels.T
        mine = tr_s[pl.ds(pl.multiple_of(lax.rem(f, per_tile) * rows_each, rows_each), rows_each), :]
        weights = []
        for i in range(2):
            level = mine[:, i * nf:(i + 1) * nf]
            e = jnp.exp(level - jnp.max(level, axis=1, keepdims=True))
            weights.append(e / jnp.sum(e, axis=1, keepdims=True))
        landed(PART, p, po_s.at[p, pl.ds(0, nf - 1)])
        first = lane((rows_each, LANES)) < HEAD_DIM
        context = jnp.zeros((rows_each, LANES), F32)
        for s in range(nf):
            w = jnp.where(first, weights[0][:, s:s + 1], weights[1][:, s:s + 1])
            context += w * po_s[p, s].astype(F32)
        return context.astype(BF16)

    def head_total(kind, slot, p, part):
        sum_s[p, slot, h] = part.astype(BF16)

        def send(d, _):
            t = lax.rem(h + d, nh)
            pltpu.make_async_remote_copy(
                sum_s.at[p, slot, h], sum_s.at[p, slot, h], send_sem.at[p, kind], recv_sem.at[p, kind],
                device_id=(f, t), device_id_type=MESH,
            ).start()
            return 0

        lax.fori_loop(1, nh, send, 0)
        landed(kind, p, sum_s.at[p, slot, pl.ds(0, nh - 1)])
        out = sum_s[p, slot, 0].astype(F32)
        for i in range(1, nh):
            out += sum_s[p, slot, i].astype(F32)
        return out

    attend_start()

    def step(j, _):
        @pl.when(j < CHUNKS)
        def _():
            arrived(L, j, block(j, left))
            arrived(R, j, block(j, right))
            ring(OA, j, block(j, left, 0), block(j, left, 0), right).start()
            ring(OB, j, block(j, right, 1), block(j, right, 1), left).start()
            ring(S_L, j, block(j, left), block(j, left), sib).start()
            ring(S_R, j, block(j, right), block(j, right), sib).start()

        @pl.when(jnp.logical_and(j >= 1, j <= CHUNKS))
        def _():
            k = j - 1
            arrived(OA, k, block(k, opp, 0))
            arrived(OB, k, block(k, opp, 1))
            ring(S_OA, k, block(k, opp, 0), block(k, opp, 0), sib).start()
            ring(S_OB, k, block(k, opp, 1), block(k, opp, 1), sib).start()

        @pl.when(j >= 2)
        def _():
            k = j - 2
            r = pl.ds(pl.multiple_of(k * chunk, chunk), chunk)
            pltpu.make_async_copy(frames.at[r, :], x_s.at[r, cols(h)], own_sem.at[k]).wait()
            for kind in (S_OWN, S_L, S_R):
                arrived(kind, k, block(k, sib))
            for part, kind in enumerate((S_OA, S_OB)):
                arrived(kind, k, block(k, sib, part))
            keys_values(k)
            attend(0, k)

        return 0

    lax.fori_loop(0, CHUNKS + 2, step, 0)

    for p in range(passes):
        if p > 0:
            attend_start()

            def again(k, _):
                attend(p, k)
                return 0

            lax.fori_loop(0, CHUNKS, again, 0)
        context = attend_end(p)
        if p == 0:
            loaded(3, co_s)
        rows = rows + head_total(CROSS, 0, p, project(context, co_s[p]))

        if p == 0:
            loaded(4, sqkv_s)
        self_qkv = project(layer_norm(rows).astype(BF16), sqkv_s[p])
        kv_s[p, own_rows, :] = self_qkv[:, LANES:].astype(BF16)
        exchange_f(KEYS, p, [(lambda t: kv_s.at[p, own_rows, :], kv_s.at[p, own_rows, :], None)])
        q = by_head((self_qkv[:, :LANES] * 0.125).astype(BF16))
        landed(KEYS, p, kv_s.at[p, pl.ds(0, latent_count - rows_each)])
        scores = against(q, kv_s[p, :, pl.ds(0, LANES)])
        e = jnp.exp(scores - jnp.max(scores, axis=1, keepdims=True))
        weight = (e / jnp.sum(e, axis=1, keepdims=True)).astype(BF16)
        both = project(weight, kv_s[p, :, pl.ds(LANES, LANES)])
        first = lane((rows_each, LANES)) < HEAD_DIM
        context = jnp.where(first, both[:rows_each], both[rows_each:]).astype(BF16)
        if p == 0:
            loaded(5, so_s)
        rows = rows + head_total(SELF, 1, p, project(context, so_s[p]))

        if p == 0:
            loaded(6, mi_s)
        u = project(layer_norm(rows).astype(BF16), mi_s[p])
        hidden = (0.5 * u * (1.0 + lax.erf(u * 0.7071067811865476))).astype(BF16)
        if p == 0:
            loaded(7, mo_s)
        rows = rows + head_total(MLP, 2, p, project(hidden, mo_s[p]))

        if p + 1 < passes:
            q = (project(layer_norm(rows).astype(BF16), cq_s[p + 1]) * 0.125).astype(BF16)
            qall_s[p + 1, own_rows, :] = q
            here = qall_s.at[p + 1, own_rows, :]
            exchange_f(QUERY, p, [(lambda t: here, here, None)])
        if p == 0:
            row_s[...] = rows
            source, there = row_s.at[:, cols(h)], mid_s.at[own_rows, :]
            exchange_f(MID, p, [(lambda t: source, there, None)])
            mid_s[own_rows, :] = row_s[:, cols(h)]
        if p + 1 < passes:
            landed(QUERY, p, qall_s.at[p + 1, pl.ds(0, latent_count - rows_each)])

    encoded[...] = rows
    landed(MID, 0, mid_s.at[pl.ds(0, latent_count - rows_each)])
    midway[...] = mid_s[...]

    ring(0, 0, x_s.at[:, pl.ds(0, 7 * LANES)], x_s.at[:, pl.ds(0, 7 * LANES)], sib).wait_send()
    for p in range(passes):
        sent(PART, p, po_s.at[p, pl.ds(0, nf - 1)])
        sent(STAT, p, ps_s.at[p, pl.ds(0, nf - 1)])
        sent(KEYS, p, kv_s.at[p, pl.ds(0, latent_count - rows_each)])
        for slot, kind in enumerate((CROSS, SELF, MLP)):
            sent(kind, p, sum_s.at[p, slot, pl.ds(0, nh - 1)])
        if p + 1 < passes:
            sent(QUERY, p, qall_s.at[p + 1, pl.ds(0, latent_count - rows_each)])
    sent(MID, 0, mid_s.at[pl.ds(0, latent_count - rows_each)])


def local(nf, nh, *args):
    frames, latents, cq, mi = args[0], args[1], args[2], args[10]
    frame_count = frames.shape[0]
    latent_count, width = latents.shape
    passes, hidden = cq.shape[0], mi.shape[2]
    rows_each = latent_count // nf
    vm = pltpu.VMEM
    scratch = [
        vm((frame_count, width), BF16),
        vm((latent_count, width), BF16),
        vm((passes, width, LANES), BF16),
        vm((width, 2 * passes * LANES), BF16),
        vm((passes, LANES, width), BF16),
        vm((passes, width, 3 * LANES), BF16),
        vm((passes, LANES, width), BF16),
        vm((passes, width, hidden), BF16),
        vm((passes, hidden, width), BF16),
        vm((passes, frame_count, LANES), BF16),
        vm((passes, LANES + ONES, frame_count), BF16),
        vm((passes, latent_count, LANES), BF16),
        vm((1, 2 * latent_count), F32),
        vm((LANES + ONES, 2 * latent_count), F32),
        vm((passes, latent_count, LANES), BF16),
        vm((passes, latent_count // LANES, 2, LANES), F32),
        vm((passes, nf, rows_each, LANES), BF16),
        vm((passes, nf, 2, LANES), F32),
        vm((LANES, 2 * nf), F32),
        vm((passes, latent_count, 2 * LANES), BF16),
        vm((passes, 3, nh, rows_each, width), BF16),
        vm((rows_each, width), F32),
        vm((latent_count, LANES), F32),
        pltpu.SemaphoreType.DMA((8,)),
        pltpu.SemaphoreType.DMA((CHUNKS,)),
        pltpu.SemaphoreType.DMA((9, CHUNKS)),
        pltpu.SemaphoreType.DMA(()),
        pltpu.SemaphoreType.DMA((passes, 8)),
        pltpu.SemaphoreType.DMA((passes, 8)),
    ]
    return pl.pallas_call(
        functools.partial(kernel, nf, nh),
        out_shape=(
            jax.ShapeDtypeStruct((rows_each, width), F32),
            jax.ShapeDtypeStruct((latent_count, LANES), F32),
        ),
        in_specs=[pl.BlockSpec(memory_space=pl.ANY)] * len(args),
        out_specs=(pl.BlockSpec(memory_space=vm), pl.BlockSpec(memory_space=vm)),
        scratch_shapes=scratch,
        compiler_params=pltpu.CompilerParams(
            collective_id=0, has_side_effects=True, vmem_limit_bytes=56 * 1024 * 1024
        ),
    )(*args)


def solution(mesh):
    nf, nh = mesh.shape["frames"], mesh.shape["heads"]
    by_column, by_row = P(None, None, "heads"), P(None, "heads", None)
    placed = (
        P("frames", "heads"), P(),
        by_column, by_column, by_column, by_row,
        by_column, by_column, by_column, by_row,
        by_column, by_row,
    )
    return jax.shard_map(
        functools.partial(local, nf, nh),
        mesh=mesh,
        in_specs=placed,
        out_specs=(P("frames", None), P(None, "heads")),
        check_vma=False,
    )
```

time: 408 us -> 114 us (0.28)
  waiting for transfers between devices: 161 us -> 0 us
  blocking collectives: 135 us -> 0 us
  Pallas kernels: 0 us -> 110 us
  starting transfers between devices: 36.8 us -> 0 us
  matrix products: 27.5 us -> 0 us
  other arithmetic: 18.3 us -> 0 us
  between operations: 14.2 us -> 0.64 us
  local copies, waits for them, and re-layouts: 14.2 us -> 3.14 us
    pallas_call x0 -> x1, Pallas kernels: none -> 110 us  [local(): pl.pallas_call(functools.partial(kernel, nf, nh), out_shape=(jax.ShapeDty...]
    all_gather x3 -> x0, waiting for transfers between devices: 103 us -> none  [gathered_by_axis(): nearer = lax.all_gather(value, axes[-1], axis=dim, tiled=True)]
    all_to_all x6 -> x0, blocking collectives: 103 us -> none  [the longest x4 69.3 us: sent_to_all(): lax.all_to_all(jnp.broadcast_to(value[None], (peers, *value.shape)), axis...]
    all_to_all x5 -> x0, waiting for transfers between devices: 57.2 us -> none  [sent_to_all(): lax.all_to_all(jnp.broadcast_to(value[None], (peers, *value.shape)), axis...]
    all_to_all x5 -> x0, starting transfers between devices: 36.7 us -> none  [sent_to_all(): lax.all_to_all(jnp.broadcast_to(value[None], (peers, *value.shape)), axis...]
    all_gather x3 -> x0, blocking collectives: 31.7 us -> none  [gathered_by_axis(): nearer = lax.all_gather(value, axes[-1], axis=dim, tiled=True)]
    dot_general x26 -> x0, matrix products: 27.5 us -> none  [the longest x18 14 us: project(): return jnp.dot(left_side, weight, preferred_element_type=jnp.float32)]
    reduce_sum x24 -> x0, other arithmetic: 15.3 us -> none  [the longest x7 6.43 us: layer_norm(): centre = vector - jnp.mean(vector, axis=-1, keepdims=True)]
  transfers between devices with their start and end apart: 8 -> 0, of which waited for: 8 -> 0; matrix products, arithmetic and copies ran while one was open for 2% -> 0% of each run, Pallas kernels for 0% -> 0%
where the time goes in v1:
time: 114 us
  Pallas kernels  110 us (96%)
  local copies, waits for them, and re-layouts  3.14 us (3%)
    pallas_call x1, Pallas kernels, local(): pl.pallas_call(functools.partial(kernel, nf, nh), out_shape=(jax.ShapeDty...  110 us
    unnamed x2, local copies, waits for them, and re-layouts  3.14 us

profile of v1, /device:TPU:1, one launch (start us, length us, event | category | flops | bytes accessed | tf_op | source)
XLA Modules:
  0.0 113.6 jit_solution(1132699625156088892)
XLA Ops:
  0.6 109.9 %shard_map.131 = (f32[16,1024]{1,0:T(8,128)}, f32[512,128]{1,0:T(8,128)}) custom-call(bf16[1024,128]{1,0:T(8,128)(2,1)} %frames.1, bf16[512,1024]{1,0:T(8,128)(2,1)} %latents.1, bf16[2,1024,128]{2,1,0:T(8,128)(2,1)} %cq.1, bf16[2,1024,128]{2,1,0:T(8,128)(2,1)} %ck.1, bf16[2,1024,128]{2,1,0:T(8,128)(2,1)} %cv.1, bf16[2,128,1024]{2,1,0:T(8,128)(2,1)} %co.1, ...), custom_call_target="tpu_custom_call" | custom-call | tf_op jit(solution)/shard_map/pallas_call | solution.py:385
  110.5 1.5 %copy.16 = f32[16,1024]{1,0:T(8,128)} copy(f32[16,1024]{1,0:T(8,128)} %get-tuple-element.4) | data formatting | bytes 131072
  112.0 1.7 %copy.17 = f32[512,128]{1,0:T(8,128)} copy(f32[512,128]{1,0:T(8,128)} %get-tuple-element.5) | data formatting | bytes 524288

commit v2 on v1

--- a/solution.py
+++ b/solution.py
@@ -15,7 +15,7 @@
 CHUNKS = 4
 LANES = 128
 ONES = 16
-PART, STAT, CROSS, KEYS, SELF, MLP, QUERY, MID = range(8)
+PART, STAT, CROSS, KEYS, VALUES, SELF, MLP, QUERY, MID = range(9)
 
 
 def layer_norm(v):
@@ -40,6 +40,11 @@
     first = lane(q.shape) < HEAD_DIM
     zero = jnp.zeros_like(q)
     return jnp.concatenate([jnp.where(first, q, zero), jnp.where(first, zero, q)], axis=0)
+
+
+def farthest_first(nz, nx):
+    steps = [(dz, dx) for dz in range(nz) for dx in range(nx) if dz or dx]
+    return sorted(steps, key=lambda s: -(min(s[0], nz - s[0]) + min(s[1], nx - s[1])))
 
 
 def kernel(
@@ -47,7 +52,7 @@
     frames, latents, cq, ck, cv, co, sq, sk, sv, so, mi, mo,
     encoded, midway,
     x_s, lat_s, cq_s, ckv_s, co_s, sqkv_s, so_s, mi_s, mo_s,
-    k_s, vt_s, qall_s, m_s, acc_s, o_s, st_s, po_s, ps_s, tr_s, kv_s, sum_s, row_s, mid_s,
+    k_s, vt_s, qall_s, qh_s, m_s, acc_s, o_s, st_s, po_s, ps_s, tr_s, sk_s, sv_s, sum_s, row_s, mid_s,
     w_sem, own_sem, ring_recv, ring_send, recv_sem, send_sem,
 ):
     f, h = lax.axis_index("frames"), lax.axis_index("heads")
@@ -91,16 +96,21 @@
 
     barrier = pltpu.get_barrier_semaphore()
 
-    def greet_f(p, _):
-        pl.semaphore_signal(barrier, inc=1, device_id=(lax.rem(f + p, nf), h), device_id_type=MESH)
-        return 0
+    nx = 4
+    nz = nf // nx
+    z, x = f // nx, lax.rem(f, nx)
+
+    def frames_peers():
+        for dz, dx in farthest_first(nz, nx):
+            yield lax.rem(z + dz, nz) * nx + lax.rem(x + dx, nx)
 
     def greet_h(p, _):
         pl.semaphore_signal(barrier, inc=1, device_id=(f, lax.rem(h + p, nh)), device_id_type=MESH)
         return 0
 
+    for t in frames_peers():
+        pl.semaphore_signal(barrier, inc=1, device_id=(t, h), device_id_type=MESH)
     lax.fori_loop(1, nh, greet_h, 0)
-    lax.fori_loop(1, nf, greet_f, 0)
     pl.semaphore_wait(barrier, nf + nh - 2)
 
     L, R, OA, OB, S_OWN, S_L, S_R, S_OA, S_OB = range(9)
@@ -126,14 +136,11 @@
 
     lax.fori_loop(0, CHUNKS, send_own, 0)
 
-    def set_queries(p, q):
-        qall_s[p] = q
-
     loaded(0, lat_s)
     loaded(1, cq_s)
     state = lat_s[...].astype(F32)
     q0 = (project(layer_norm(state).astype(BF16), cq_s[0]) * 0.125).astype(BF16)
-    set_queries(0, q0)
+    qh_s[...] = by_head(q0)
     rows = lat_s[own_rows, :].astype(F32)
     for p in range(passes):
         vt_s[p, pl.ds(LANES, ONES), :] = jnp.ones((ONES, frame_count), BF16)
@@ -154,23 +161,22 @@
 
     def attend(p, k):
         r = pl.ds(pl.multiple_of(k * chunk, chunk), chunk)
-        scores = against(k_s[p, r, :], by_head(qall_s[p]))
+        scores = against(k_s[p, r, :], qh_s[...])
         before = m_s[...]
         highest = jnp.maximum(before, jnp.max(scores, axis=0, keepdims=True))
         terms = jnp.exp(scores - highest).astype(BF16)
         acc_s[...] = acc_s[...] * jnp.exp(before - highest) + project(vt_s[p, :, r], terms)
         m_s[...] = highest
 
-    def exchange_f(kind, p, pairs):
-        def send(d, _):
-            t = lax.rem(f + d, nf)
-            for i, (src_of, dst, _all) in enumerate(pairs):
-                pltpu.make_async_remote_copy(
-                    src_of(t), dst, send_sem.at[p, kind + i], recv_sem.at[p, kind + i],
-                    device_id=(t, h), device_id_type=MESH,
-                ).start()
-            return 0
-        lax.fori_loop(1, nf, send, 0)
+    outstanding = []
+
+    def exchange_f(kind, p, source, there, everything):
+        for t in frames_peers():
+            pltpu.make_async_remote_copy(
+                source(t), there, send_sem.at[p, kind], recv_sem.at[p, kind],
+                device_id=(t, h), device_id_type=MESH,
+            ).start()
+        outstanding.append(lambda: sent(kind, p, everything))
 
     def landed(kind, p, ref):
         pltpu.make_async_remote_copy(
@@ -199,13 +205,12 @@
             return pl.ds(pl.multiple_of(t * rows_each, rows_each), rows_each)
 
         per_tile = LANES // rows_each
-        exchange_f(PART, p, [
-            (lambda t: o_s.at[p, rows_of(t), :], po_s.at[p, f], None),
-            (lambda t: st_s.at[p, t // per_tile], ps_s.at[p, f], None),
-        ])
+        stats, parts = ps_s.at[p, pl.ds(0, nf - 1)], po_s.at[p, pl.ds(0, nf - 1)]
+        exchange_f(STAT, p, lambda t: st_s.at[p, t // per_tile], ps_s.at[p, f], stats)
+        exchange_f(PART, p, lambda t: o_s.at[p, rows_of(t), :], po_s.at[p, f], parts)
         po_s[p, f] = o_s[p, own_rows, :]
         ps_s[p, f] = st_s[p, f // per_tile]
-        landed(STAT, p, ps_s.at[p, pl.ds(0, nf - 1)])
+        landed(STAT, p, stats)
         levels = jnp.concatenate([ps_s[p, :, 0, :], ps_s[p, :, 1, :]], axis=0)
         tr_s[...] = levels.T
         mine = tr_s[pl.ds(pl.multiple_of(lax.rem(f, per_tile) * rows_each, rows_each), rows_each), :]
@@ -214,7 +219,7 @@
             level = mine[:, i * nf:(i + 1) * nf]
             e = jnp.exp(level - jnp.max(level, axis=1, keepdims=True))
             weights.append(e / jnp.sum(e, axis=1, keepdims=True))
-        landed(PART, p, po_s.at[p, pl.ds(0, nf - 1)])
+        landed(PART, p, parts)
         first = lane((rows_each, LANES)) < HEAD_DIM
         context = jnp.zeros((rows_each, LANES), F32)
         for s in range(nf):
@@ -234,6 +239,7 @@
             return 0
 
         lax.fori_loop(1, nh, send, 0)
+        outstanding.append(lambda: sent(kind, p, sum_s.at[p, slot, pl.ds(0, nh - 1)]))
         landed(kind, p, sum_s.at[p, slot, pl.ds(0, nh - 1)])
         out = sum_s[p, slot, 0].astype(F32)
         for i in range(1, nh):
@@ -279,6 +285,7 @@
     for p in range(passes):
         if p > 0:
             attend_start()
+            qh_s[...] = by_head(qall_s[p])
 
             def again(k, _):
                 attend(p, k)
@@ -293,14 +300,18 @@
         if p == 0:
             loaded(4, sqkv_s)
         self_qkv = project(layer_norm(rows).astype(BF16), sqkv_s[p])
-        kv_s[p, own_rows, :] = self_qkv[:, LANES:].astype(BF16)
-        exchange_f(KEYS, p, [(lambda t: kv_s.at[p, own_rows, :], kv_s.at[p, own_rows, :], None)])
+        others = pl.ds(0, latent_count - rows_each)
+        for i, (kind, ref) in enumerate(((KEYS, sk_s), (VALUES, sv_s))):
+            ref[p, own_rows, :] = self_qkv[:, (i + 1) * LANES:(i + 2) * LANES].astype(BF16)
+            here = ref.at[p, own_rows, :]
+            exchange_f(kind, p, lambda t: here, here, ref.at[p, others, :])
         q = by_head((self_qkv[:, :LANES] * 0.125).astype(BF16))
-        landed(KEYS, p, kv_s.at[p, pl.ds(0, latent_count - rows_each)])
-        scores = against(q, kv_s[p, :, pl.ds(0, LANES)])
+        landed(KEYS, p, sk_s.at[p, others, :])
+        scores = against(q, sk_s[p])
         e = jnp.exp(scores - jnp.max(scores, axis=1, keepdims=True))
         weight = (e / jnp.sum(e, axis=1, keepdims=True)).astype(BF16)
-        both = project(weight, kv_s[p, :, pl.ds(LANES, LANES)])
+        landed(VALUES, p, sv_s.at[p, others, :])
+        both = project(weight, sv_s[p])
         first = lane((rows_each, LANES)) < HEAD_DIM
         context = jnp.where(first, both[:rows_each], both[rows_each:]).astype(BF16)
         if p == 0:
@@ -319,29 +330,22 @@
             q = (project(layer_norm(rows).astype(BF16), cq_s[p + 1]) * 0.125).astype(BF16)
             qall_s[p + 1, own_rows, :] = q
             here = qall_s.at[p + 1, own_rows, :]
-            exchange_f(QUERY, p, [(lambda t: here, here, None)])
+            exchange_f(QUERY, p, lambda t: here, here, qall_s.at[p + 1, others, :])
         if p == 0:
             row_s[...] = rows
             source, there = row_s.at[:, cols(h)], mid_s.at[own_rows, :]
-            exchange_f(MID, p, [(lambda t: source, there, None)])
+            exchange_f(MID, p, lambda t: source, there, mid_s.at[others, :])
             mid_s[own_rows, :] = row_s[:, cols(h)]
         if p + 1 < passes:
-            landed(QUERY, p, qall_s.at[p + 1, pl.ds(0, latent_count - rows_each)])
+            landed(QUERY, p, qall_s.at[p + 1, others, :])
 
     encoded[...] = rows
     landed(MID, 0, mid_s.at[pl.ds(0, latent_count - rows_each)])
     midway[...] = mid_s[...]
 
     ring(0, 0, x_s.at[:, pl.ds(0, 7 * LANES)], x_s.at[:, pl.ds(0, 7 * LANES)], sib).wait_send()
-    for p in range(passes):
-        sent(PART, p, po_s.at[p, pl.ds(0, nf - 1)])
-        sent(STAT, p, ps_s.at[p, pl.ds(0, nf - 1)])
-        sent(KEYS, p, kv_s.at[p, pl.ds(0, latent_count - rows_each)])
-        for slot, kind in enumerate((CROSS, SELF, MLP)):
-            sent(kind, p, sum_s.at[p, slot, pl.ds(0, nh - 1)])
-        if p + 1 < passes:
-            sent(QUERY, p, qall_s.at[p + 1, pl.ds(0, latent_count - rows_each)])
-    sent(MID, 0, mid_s.at[pl.ds(0, latent_count - rows_each)])
+    for wait in outstanding:
+        wait()
 
 
 def local(nf, nh, *args):
@@ -364,6 +368,7 @@
         vm((passes, frame_count, LANES), BF16),
         vm((passes, LANES + ONES, frame_count), BF16),
         vm((passes, latent_count, LANES), BF16),
+        vm((2 * latent_count, LANES), BF16),
         vm((1, 2 * latent_count), F32),
         vm((LANES + ONES, 2 * latent_count), F32),
         vm((passes, latent_count, LANES), BF16),
@@ -371,7 +376,8 @@
         vm((passes, nf, rows_each, LANES), BF16),
         vm((passes, nf, 2, LANES), F32),
         vm((LANES, 2 * nf), F32),
-        vm((passes, latent_count, 2 * LANES), BF16),
+        vm((passes, latent_count, LANES), BF16),
+        vm((passes, latent_count, LANES), BF16),
         vm((passes, 3, nh, rows_each, width), BF16),
         vm((rows_each, width), F32),
         vm((latent_count, LANES), F32),
@@ -379,8 +385,8 @@
         pltpu.SemaphoreType.DMA((CHUNKS,)),
         pltpu.SemaphoreType.DMA((9, CHUNKS)),
         pltpu.SemaphoreType.DMA(()),
-        pltpu.SemaphoreType.DMA((passes, 8)),
-        pltpu.SemaphoreType.DMA((passes, 8)),
+        pltpu.SemaphoreType.DMA((passes, 9)),
+        pltpu.SemaphoreType.DMA((passes, 9)),
     ]
     return pl.pallas_call(
         functools.partial(kernel, nf, nh),

time: 114 us -> 108 us (0.947)
  Pallas kernels: 110 us -> 105 us
    pallas_call x1, Pallas kernels: 110 us -> 105 us  [local(): pl.pallas_call(functools.partial(kernel, nf, nh), out_shape=(jax.ShapeDty...]
where the time goes in v2:
time: 108 us
  Pallas kernels  105 us (97%)
  local copies, waits for them, and re-layouts  3.14 us (3%)
    pallas_call x1, Pallas kernels, local(): pl.pallas_call(functools.partial(kernel, nf, nh), out_shape=(jax.ShapeDty...  105 us
    unnamed x2, local copies, waits for them, and re-layouts  3.14 us

profile of v2, /device:TPU:1, one launch (start us, length us, event | category | flops | bytes accessed | tf_op | source)
XLA Modules:
  0.0 108.3 jit_solution(8741069093775968918)
XLA Ops:
  0.6 104.6 %shard_map.131 = (f32[16,1024]{1,0:T(8,128)}, f32[512,128]{1,0:T(8,128)}) custom-call(bf16[1024,128]{1,0:T(8,128)(2,1)} %frames.1, bf16[512,1024]{1,0:T(8,128)(2,1)} %latents.1, bf16[2,1024,128]{2,1,0:T(8,128)(2,1)} %cq.1, bf16[2,1024,128]{2,1,0:T(8,128)(2,1)} %ck.1, bf16[2,1024,128]{2,1,0:T(8,128)(2,1)} %cv.1, bf16[2,128,1024]{2,1,0:T(8,128)(2,1)} %co.1, ...), custom_call_target="tpu_custom_call" | custom-call | tf_op jit(solution)/shard_map/pallas_call | solution.py:391
  105.2 1.5 %copy.16 = f32[16,1024]{1,0:T(8,128)} copy(f32[16,1024]{1,0:T(8,128)} %get-tuple-element.4) | data formatting | bytes 131072
  106.7 1.7 %copy.17 = f32[512,128]{1,0:T(8,128)} copy(f32[512,128]{1,0:T(8,128)} %get-tuple-element.5) | data formatting | bytes 524288

commit v3 on v2

--- a/solution.py
+++ b/solution.py
@@ -15,7 +15,8 @@
 CHUNKS = 4
 LANES = 128
 ONES = 16
-PART, STAT, CROSS, KEYS, VALUES, SELF, MLP, QUERY, MID = range(9)
+PART, STAT, KEYS, VALUES, QUERY, MID, CROSS, SELF, MLP = range(9)
+PAIRS = 3
 
 
 def layer_norm(v):
@@ -52,7 +53,7 @@
     frames, latents, cq, ck, cv, co, sq, sk, sv, so, mi, mo,
     encoded, midway,
     x_s, lat_s, cq_s, ckv_s, co_s, sqkv_s, so_s, mi_s, mo_s,
-    k_s, vt_s, qall_s, qh_s, m_s, acc_s, o_s, st_s, po_s, ps_s, tr_s, sk_s, sv_s, sum_s, row_s, mid_s,
+    k_s, vt_s, qall_s, qh_s, m_s, acc_s, o_s, st_s, po_s, ps_s, tr_s, sk_s, sv_s, give_s, take_s, sum_s, row_s, mid_s,
     w_sem, own_sem, ring_recv, ring_send, recv_sem, send_sem,
 ):
     f, h = lax.axis_index("frames"), lax.axis_index("heads")
@@ -60,7 +61,7 @@
     frame_count = x_s.shape[0]
     rows_each = latent_count // nf
     chunk = frame_count // CHUNKS
-    half = chunk // 2
+    half = width // 2
     passes = cq_s.shape[0]
 
     sib = h + 1 - 2 * lax.rem(h, 2)
@@ -113,28 +114,28 @@
     lax.fori_loop(1, nh, greet_h, 0)
     pl.semaphore_wait(barrier, nf + nh - 2)
 
-    L, R, OA, OB, S_OWN, S_L, S_R, S_OA, S_OB = range(9)
+    L, R, O, S_OWN, S_L, S_R, S_O = range(7)
 
     def ring(kind, k, src, dst, to):
         return pltpu.make_async_remote_copy(
             src, dst, ring_send, ring_recv.at[kind, k], device_id=(f, to), device_id_type=MESH
         )
 
-    def block(k, who, part=None):
-        start, size = (k * chunk, chunk) if part is None else (k * chunk + part * half, half)
-        return x_s.at[pl.ds(pl.multiple_of(start, half), size), cols(who)]
-
-    def arrived(kind, k, ref):
-        ring(kind, k, ref, ref, sib).wait_recv()
-
-    def send_own(k, _):
-        src = frames.at[pl.ds(pl.multiple_of(k * chunk, chunk), chunk), :]
-        ring(L, k, src, block(k, h), right).start()
-        ring(R, k, src, block(k, h), left).start()
-        ring(S_OWN, k, src, block(k, h), sib).start()
-        return 0
-
-    lax.fori_loop(0, CHUNKS, send_own, 0)
+    def block(k, who):
+        return x_s.at[pl.ds(k * chunk, chunk), cols(who)]
+
+    def arrived(kind, k, who):
+        ring(kind, k, block(k, who), block(k, who), sib).wait_recv()
+
+    def pass_on(kind, k, who, to):
+        ring(kind, k, block(k, who), block(k, who), to).start()
+
+    evens, odds = range(0, CHUNKS, 2), range(1, CHUNKS, 2)
+    for a, b in zip((*evens, *odds), (*odds, *evens)):
+        for kind, k, to in ((L, a, right), (R, b, left)):
+            ring(kind, k, frames.at[pl.ds(k * chunk, chunk), :], block(k, h), to).start()
+    for k in range(CHUNKS):
+        ring(S_OWN, k, frames.at[pl.ds(k * chunk, chunk), :], block(k, h), sib).start()
 
     loaded(0, lat_s)
     loaded(1, cq_s)
@@ -147,7 +148,7 @@
     loaded(2, ckv_s)
 
     def keys_values(k):
-        r = pl.ds(pl.multiple_of(k * chunk, chunk), chunk)
+        r = pl.ds(k * chunk, chunk)
         normed = layer_norm(x_s[r, :].astype(F32)).astype(BF16)
         both = project(normed, ckv_s[...])
         for p in range(passes):
@@ -227,60 +228,59 @@
             context += w * po_s[p, s].astype(F32)
         return context.astype(BF16)
 
-    def head_total(kind, slot, p, part):
-        sum_s[p, slot, h] = part.astype(BF16)
-
-        def send(d, _):
-            t = lax.rem(h + d, nh)
+    core = lax.rem(h, 2)
+
+    def half_of(c):
+        return pl.ds(pl.multiple_of(c * half, half), half)
+
+    def head_total(kind, slot, p, left_side, weight):
+        give_s[p, slot] = project(left_side, weight[p, :, half_of(1 - core)]).astype(BF16)
+        pair = pltpu.make_async_remote_copy(
+            give_s.at[p, slot], take_s.at[p, slot], send_sem.at[p, kind + PAIRS], recv_sem.at[p, kind + PAIRS],
+            device_id=(f, sib), device_id_type=MESH,
+        )
+        pair.start()
+        mine = project(left_side, weight[p, :, half_of(core)])
+        pair.wait()
+        sum_s[p, slot, h] = (mine + take_s[p, slot].astype(F32)).astype(BF16)
+        for d in (4, 5, 3, 2, 6, 7, 1):
             pltpu.make_async_remote_copy(
                 sum_s.at[p, slot, h], sum_s.at[p, slot, h], send_sem.at[p, kind], recv_sem.at[p, kind],
-                device_id=(f, t), device_id_type=MESH,
+                device_id=(f, lax.rem(h + d, nh)), device_id_type=MESH,
             ).start()
-            return 0
-
-        lax.fori_loop(1, nh, send, 0)
         outstanding.append(lambda: sent(kind, p, sum_s.at[p, slot, pl.ds(0, nh - 1)]))
         landed(kind, p, sum_s.at[p, slot, pl.ds(0, nh - 1)])
-        out = sum_s[p, slot, 0].astype(F32)
-        for i in range(1, nh):
-            out += sum_s[p, slot, i].astype(F32)
-        return out
+        halves = []
+        for c in range(2):
+            out = sum_s[p, slot, c].astype(F32)
+            for i in range(c + 2, nh, 2):
+                out += sum_s[p, slot, i].astype(F32)
+            halves.append(out)
+        return jnp.concatenate(halves, axis=1)
 
     attend_start()
 
-    def step(j, _):
-        @pl.when(j < CHUNKS)
-        def _():
-            arrived(L, j, block(j, left))
-            arrived(R, j, block(j, right))
-            ring(OA, j, block(j, left, 0), block(j, left, 0), right).start()
-            ring(OB, j, block(j, right, 1), block(j, right, 1), left).start()
-            ring(S_L, j, block(j, left), block(j, left), sib).start()
-            ring(S_R, j, block(j, right), block(j, right), sib).start()
-
-        @pl.when(jnp.logical_and(j >= 1, j <= CHUNKS))
-        def _():
+    for k in range(CHUNKS):
+        kind, onward, who, to = (L, S_L, left, right) if k % 2 == 0 else (R, S_R, right, left)
+        arrived(kind, k, who)
+        pass_on(O, k, who, to)
+        pass_on(onward, k, who, sib)
+    for k in (*odds, *evens):
+        kind, onward, who = (R, S_R, right) if k % 2 == 0 else (L, S_L, left)
+        arrived(kind, k, who)
+        pass_on(onward, k, who, sib)
+    for j in range(CHUNKS + 1):
+        if j < CHUNKS:
+            arrived(O, j, opp)
+            pass_on(S_O, j, opp, sib)
+        if j > 0:
             k = j - 1
-            arrived(OA, k, block(k, opp, 0))
-            arrived(OB, k, block(k, opp, 1))
-            ring(S_OA, k, block(k, opp, 0), block(k, opp, 0), sib).start()
-            ring(S_OB, k, block(k, opp, 1), block(k, opp, 1), sib).start()
-
-        @pl.when(j >= 2)
-        def _():
-            k = j - 2
-            r = pl.ds(pl.multiple_of(k * chunk, chunk), chunk)
+            r = pl.ds(k * chunk, chunk)
             pltpu.make_async_copy(frames.at[r, :], x_s.at[r, cols(h)], own_sem.at[k]).wait()
-            for kind in (S_OWN, S_L, S_R):
-                arrived(kind, k, block(k, sib))
-            for part, kind in enumerate((S_OA, S_OB)):
-                arrived(kind, k, block(k, sib, part))
+            for kind in (S_OWN, S_L, S_R, S_O):
+                arrived(kind, k, sib)
             keys_values(k)
             attend(0, k)
-
-        return 0
-
-    lax.fori_loop(0, CHUNKS + 2, step, 0)
 
     for p in range(passes):
         if p > 0:
@@ -295,17 +295,17 @@
         context = attend_end(p)
         if p == 0:
             loaded(3, co_s)
-        rows = rows + head_total(CROSS, 0, p, project(context, co_s[p]))
+        rows = rows + head_total(CROSS, 0, p, context, co_s)
 
         if p == 0:
             loaded(4, sqkv_s)
-        self_qkv = project(layer_norm(rows).astype(BF16), sqkv_s[p])
+        self_in = layer_norm(rows).astype(BF16)
         others = pl.ds(0, latent_count - rows_each)
         for i, (kind, ref) in enumerate(((KEYS, sk_s), (VALUES, sv_s))):
-            ref[p, own_rows, :] = self_qkv[:, (i + 1) * LANES:(i + 2) * LANES].astype(BF16)
+            ref[p, own_rows, :] = project(self_in, sqkv_s[p, :, pl.ds((i + 1) * LANES, LANES)]).astype(BF16)
             here = ref.at[p, own_rows, :]
             exchange_f(kind, p, lambda t: here, here, ref.at[p, others, :])
-        q = by_head((self_qkv[:, :LANES] * 0.125).astype(BF16))
+        q = by_head((project(self_in, sqkv_s[p, :, pl.ds(0, LANES)]) * 0.125).astype(BF16))
         landed(KEYS, p, sk_s.at[p, others, :])
         scores = against(q, sk_s[p])
         e = jnp.exp(scores - jnp.max(scores, axis=1, keepdims=True))
@@ -316,7 +316,7 @@
         context = jnp.where(first, both[:rows_each], both[rows_each:]).astype(BF16)
         if p == 0:
             loaded(5, so_s)
-        rows = rows + head_total(SELF, 1, p, project(context, so_s[p]))
+        rows = rows + head_total(SELF, 1, p, context, so_s)
 
         if p == 0:
             loaded(6, mi_s)
@@ -324,7 +324,7 @@
         hidden = (0.5 * u * (1.0 + lax.erf(u * 0.7071067811865476))).astype(BF16)
         if p == 0:
             loaded(7, mo_s)
-        rows = rows + head_total(MLP, 2, p, project(hidden, mo_s[p]))
+        rows = rows + head_total(MLP, 2, p, hidden, mo_s)
 
         if p + 1 < passes:
             q = (project(layer_norm(rows).astype(BF16), cq_s[p + 1]) * 0.125).astype(BF16)
@@ -378,15 +378,17 @@
         vm((LANES, 2 * nf), F32),
         vm((passes, latent_count, LANES), BF16),
         vm((passes, latent_count, LANES), BF16),
-        vm((passes, 3, nh, rows_each, width), BF16),
+        vm((passes, 3, rows_each, width // 2), BF16),
+        vm((passes, 3, rows_each, width // 2), BF16),
+        vm((passes, 3, nh, rows_each, width // 2), BF16),
         vm((rows_each, width), F32),
         vm((latent_count, LANES), F32),
         pltpu.SemaphoreType.DMA((8,)),
         pltpu.SemaphoreType.DMA((CHUNKS,)),
-        pltpu.SemaphoreType.DMA((9, CHUNKS)),
+        pltpu.SemaphoreType.DMA((7, CHUNKS)),
         pltpu.SemaphoreType.DMA(()),
-        pltpu.SemaphoreType.DMA((passes, 9)),
-        pltpu.SemaphoreType.DMA((passes, 9)),
+        pltpu.SemaphoreType.DMA((passes, 12)),
+        pltpu.SemaphoreType.DMA((passes, 12)),
     ]
     return pl.pallas_call(
         functools.partial(kernel, nf, nh),

time: 108 us -> 108 us (level)
  no operation moved by 1% of the time
where the time goes in v3:
time: 108 us
  Pallas kernels  105 us (97%)
  local copies, waits for them, and re-layouts  3.14 us (3%)
    pallas_call x1, Pallas kernels, local(): pl.pallas_call(functools.partial(kernel, nf, nh), out_shape=(jax.ShapeDty...  105 us
    unnamed x2, local copies, waits for them, and re-layouts  3.14 us

profile of v3, /device:TPU:1, one launch (start us, length us, event | category | flops | bytes accessed | tf_op | source)
XLA Modules:
  0.0 108.3 jit_solution(3109267868473603963)
XLA Ops:
  0.6 104.5 %shard_map.131 = (f32[16,1024]{1,0:T(8,128)}, f32[512,128]{1,0:T(8,128)}) custom-call(bf16[1024,128]{1,0:T(8,128)(2,1)} %frames.1, bf16[512,1024]{1,0:T(8,128)(2,1)} %latents.1, bf16[2,1024,128]{2,1,0:T(8,128)(2,1)} %cq.1, bf16[2,1024,128]{2,1,0:T(8,128)(2,1)} %ck.1, bf16[2,1024,128]{2,1,0:T(8,128)(2,1)} %cv.1, bf16[2,128,1024]{2,1,0:T(8,128)(2,1)} %co.1, ...), custom_call_target="tpu_custom_call" | custom-call | tf_op jit(solution)/shard_map/pallas_call | solution.py:393
  105.2 1.5 %copy.16 = f32[16,1024]{1,0:T(8,128)} copy(f32[16,1024]{1,0:T(8,128)} %get-tuple-element.4) | data formatting | bytes 131072
  106.6 1.7 %copy.17 = f32[512,128]{1,0:T(8,128)} copy(f32[512,128]{1,0:T(8,128)} %get-tuple-element.5) | data formatting | bytes 524288

commit v4 on v3

--- a/solution.py
+++ b/solution.py
@@ -13,6 +13,8 @@
 F32 = jnp.float32
 BF16 = jnp.bfloat16
 CHUNKS = 4
+PIECES = 8
+AHEAD = 5
 LANES = 128
 ONES = 16
 PART, STAT, KEYS, VALUES, QUERY, MID, CROSS, SELF, MLP = range(9)
@@ -61,6 +63,7 @@
     frame_count = x_s.shape[0]
     rows_each = latent_count // nf
     chunk = frame_count // CHUNKS
+    piece = frame_count // PIECES
     half = width // 2
     passes = cq_s.shape[0]
 
@@ -72,6 +75,23 @@
 
     own_rows = pl.ds(pl.multiple_of(f * rows_each, rows_each), rows_each)
 
+    barrier = pltpu.get_barrier_semaphore()
+
+    nx = 4
+    nz = nf // nx
+    z, x = f // nx, lax.rem(f, nx)
+
+    def frames_peers():
+        for dz, dx in farthest_first(nz, nx):
+            yield lax.rem(z + dz, nz) * nx + lax.rem(x + dx, nx)
+
+    def greet_h(p, _):
+        pl.semaphore_signal(barrier, inc=1, device_id=(f, lax.rem(h + p, nh)), device_id_type=MESH)
+        return 0
+
+    for t in frames_peers():
+        pl.semaphore_signal(barrier, inc=1, device_id=(t, h), device_id_type=MESH)
+    lax.fori_loop(1, nh, greet_h, 0)
     def local_copies():
         groups = [
             [(latents, lat_s)],
@@ -85,9 +105,8 @@
         ]
         return groups
 
-    for k in range(CHUNKS):
-        r = pl.ds(k * chunk, chunk)
-        pltpu.make_async_copy(frames.at[r, :], x_s.at[r, cols(h)], own_sem.at[k]).start()
+    own_block = pltpu.make_async_copy(frames, x_s.at[:, cols(h)], own_sem)
+    own_block.start()
     for i, group in enumerate(local_copies()):
         for src, dst in group:
             pltpu.make_async_copy(src, dst, w_sem.at[i]).start()
@@ -95,23 +114,6 @@
     def loaded(i, ref):
         pltpu.make_async_copy(ref, ref, w_sem.at[i]).wait()
 
-    barrier = pltpu.get_barrier_semaphore()
-
-    nx = 4
-    nz = nf // nx
-    z, x = f // nx, lax.rem(f, nx)
-
-    def frames_peers():
-        for dz, dx in farthest_first(nz, nx):
-            yield lax.rem(z + dz, nz) * nx + lax.rem(x + dx, nx)
-
-    def greet_h(p, _):
-        pl.semaphore_signal(barrier, inc=1, device_id=(f, lax.rem(h + p, nh)), device_id_type=MESH)
-        return 0
-
-    for t in frames_peers():
-        pl.semaphore_signal(barrier, inc=1, device_id=(t, h), device_id_type=MESH)
-    lax.fori_loop(1, nh, greet_h, 0)
     pl.semaphore_wait(barrier, nf + nh - 2)
 
     L, R, O, S_OWN, S_L, S_R, S_O = range(7)
@@ -122,7 +124,7 @@
         )
 
     def block(k, who):
-        return x_s.at[pl.ds(k * chunk, chunk), cols(who)]
+        return x_s.at[pl.ds(k * piece, piece), cols(who)]
 
     def arrived(kind, k, who):
         ring(kind, k, block(k, who), block(k, who), sib).wait_recv()
@@ -130,12 +132,14 @@
     def pass_on(kind, k, who, to):
         ring(kind, k, block(k, who), block(k, who), to).start()
 
-    evens, odds = range(0, CHUNKS, 2), range(1, CHUNKS, 2)
-    for a, b in zip((*evens, *odds), (*odds, *evens)):
-        for kind, k, to in ((L, a, right), (R, b, left)):
-            ring(kind, k, frames.at[pl.ds(k * chunk, chunk), :], block(k, h), to).start()
-    for k in range(CHUNKS):
-        ring(S_OWN, k, frames.at[pl.ds(k * chunk, chunk), :], block(k, h), sib).start()
+    def send_own(k):
+        src = frames.at[pl.ds(k * piece, piece), :]
+        ring(L, k, src, block(k, h), right).start()
+        ring(R, k, src, block(k, h), left).start()
+        ring(S_OWN, k, src, block(k, h), sib).start()
+
+    for k in range(AHEAD):
+        send_own(k)
 
     loaded(0, lat_s)
     loaded(1, cq_s)
@@ -260,27 +264,39 @@
 
     attend_start()
 
-    for k in range(CHUNKS):
-        kind, onward, who, to = (L, S_L, left, right) if k % 2 == 0 else (R, S_R, right, left)
-        arrived(kind, k, who)
-        pass_on(O, k, who, to)
-        pass_on(onward, k, who, sib)
-    for k in (*odds, *evens):
-        kind, onward, who = (R, S_R, right) if k % 2 == 0 else (L, S_L, left)
-        arrived(kind, k, who)
-        pass_on(onward, k, who, sib)
-    for j in range(CHUNKS + 1):
-        if j < CHUNKS:
-            arrived(O, j, opp)
-            pass_on(S_O, j, opp, sib)
-        if j > 0:
-            k = j - 1
-            r = pl.ds(k * chunk, chunk)
-            pltpu.make_async_copy(frames.at[r, :], x_s.at[r, cols(h)], own_sem.at[k]).wait()
+    def neighbours(k):
+        onward = ((L, left, right), (R, right, left))[k % 2]
+        arrived(L, k, left)
+        arrived(R, k, right)
+        pass_on(O, k, onward[1], onward[2])
+        if k + AHEAD < PIECES:
+            send_own(k + AHEAD)
+        pass_on(S_L, k, left, sib)
+        pass_on(S_R, k, right, sib)
+
+    def opposite(k):
+        arrived(O, k, opp)
+        pass_on(S_O, k, opp, sib)
+
+    def complete(c):
+        per = PIECES // CHUNKS
+        for k in range(c * per, (c + 1) * per):
             for kind in (S_OWN, S_L, S_R, S_O):
                 arrived(kind, k, sib)
-            keys_values(k)
-            attend(0, k)
+        keys_values(c)
+        attend(0, c)
+
+    own_block.wait()
+    lag = 4
+    for j in range(PIECES + lag):
+        if j < PIECES:
+            neighbours(j)
+        if j >= lag:
+            opposite(j - lag)
+        done = j - lag - 1
+        if done >= 0 and done % 2 == 1:
+            complete(done // 2)
+    complete(CHUNKS - 1)
 
     for p in range(passes):
         if p > 0:
@@ -292,6 +308,10 @@
                 return 0
 
             lax.fori_loop(0, CHUNKS, again, 0)
+        if p == 1:
+            landed(MID, 0, mid_s.at[pl.ds(0, latent_count - rows_each)])
+            mid_out = pltpu.make_async_copy(mid_s, midway, own_sem)
+            mid_out.start()
         context = attend_end(p)
         if p == 0:
             loaded(3, co_s)
@@ -340,12 +360,19 @@
             landed(QUERY, p, qall_s.at[p + 1, others, :])
 
     encoded[...] = rows
-    landed(MID, 0, mid_s.at[pl.ds(0, latent_count - rows_each)])
-    midway[...] = mid_s[...]
+    mid_out.wait()
 
     ring(0, 0, x_s.at[:, pl.ds(0, 7 * LANES)], x_s.at[:, pl.ds(0, 7 * LANES)], sib).wait_send()
     for wait in outstanding:
         wait()
+
+
+def hand_over(a, b, a_out, b_out, sem):
+    copies = [pltpu.make_async_copy(x, y, sem.at[i]) for i, (x, y) in enumerate(((a, a_out), (b, b_out)))]
+    for c in copies:
+        c.start()
+    for c in copies:
+        c.wait()
 
 
 def local(nf, nh, *args):
@@ -384,25 +411,32 @@
         vm((rows_each, width), F32),
         vm((latent_count, LANES), F32),
         pltpu.SemaphoreType.DMA((8,)),
-        pltpu.SemaphoreType.DMA((CHUNKS,)),
-        pltpu.SemaphoreType.DMA((7, CHUNKS)),
+        pltpu.SemaphoreType.DMA(()),
+        pltpu.SemaphoreType.DMA((7, PIECES)),
         pltpu.SemaphoreType.DMA(()),
         pltpu.SemaphoreType.DMA((passes, 12)),
         pltpu.SemaphoreType.DMA((passes, 12)),
     ]
-    return pl.pallas_call(
+    outs = pl.pallas_call(
         functools.partial(kernel, nf, nh),
         out_shape=(
             jax.ShapeDtypeStruct((rows_each, width), F32),
             jax.ShapeDtypeStruct((latent_count, LANES), F32),
         ),
         in_specs=[pl.BlockSpec(memory_space=pl.ANY)] * len(args),
-        out_specs=(pl.BlockSpec(memory_space=vm), pl.BlockSpec(memory_space=vm)),
+        out_specs=(pl.BlockSpec(memory_space=vm), pl.BlockSpec(memory_space=pl.ANY)),
         scratch_shapes=scratch,
         compiler_params=pltpu.CompilerParams(
             collective_id=0, has_side_effects=True, vmem_limit_bytes=56 * 1024 * 1024
         ),
     )(*args)
+    return pl.pallas_call(
+        hand_over,
+        out_shape=tuple(jax.ShapeDtypeStruct(a.shape, a.dtype) for a in outs),
+        in_specs=[pl.BlockSpec(memory_space=pl.ANY)] * 2,
+        out_specs=[pl.BlockSpec(memory_space=pl.ANY)] * 2,
+        scratch_shapes=[pltpu.SemaphoreType.DMA((2,))],
+    )(*outs)
 
 
 def solution(mesh):

time: 108 us -> 120 us (1.11)
  Pallas kernels: 105 us -> 119 us
  local copies, waits for them, and re-layouts: 3.14 us -> 0 us
    pallas_call x0 -> x1, Pallas kernels: none -> 11 us  [local(): pl.pallas_call(hand_over, out_shape=tuple((jax.ShapeDtypeStruct(a.shape,...]
    pallas_call x1, Pallas kernels: 105 us -> 108 us  [local(): pl.pallas_call(functools.partial(kernel, nf, nh), out_shape=(jax.ShapeDty...]
    unnamed x2 -> x0, local copies, waits for them, and re-layouts: 3.14 us -> none
where the time goes in v4:
time: 120 us
  Pallas kernels  119 us (99%)
    pallas_call x1, Pallas kernels, local(): pl.pallas_call(functools.partial(kernel, nf, nh), out_shape=(jax.ShapeDty...  108 us
    pallas_call x1, Pallas kernels, local(): pl.pallas_call(hand_over, out_shape=tuple((jax.ShapeDtypeStruct(a.shape,...  11 us

profile of v4, /device:TPU:1, one launch (start us, length us, event | category | flops | bytes accessed | tf_op | source)
XLA Modules:
  0.0 120.1 jit_solution(6629957593541979821)
XLA Ops:
  0.6 108.4 %shard_map.131 = (f32[16,1024]{1,0:T(8,128)}, f32[512,128]{1,0:T(8,128)}) custom-call(bf16[1024,128]{1,0:T(8,128)(2,1)} %frames.1, bf16[512,1024]{1,0:T(8,128)(2,1)} %latents.1, bf16[2,1024,128]{2,1,0:T(8,128)(2,1)} %cq.1, bf16[2,1024,128]{2,1,0:T(8,128)(2,1)} %ck.1, bf16[2,1024,128]{2,1,0:T(8,128)(2,1)} %cv.1, bf16[2,128,1024]{2,1,0:T(8,128)(2,1)} %co.1, ...), custom_call_target="tpu_custom_call" | custom-call | tf_op jit(solution)/shard_map/pallas_call | solution.py:420
  109.0 11.0 %shard_map.132 = (f32[16,1024]{1,0:T(8,128)}, f32[512,128]{1,0:T(8,128)}) custom-call(f32[16,1024]{1,0:T(8,128)} %get-tuple-element.4.a, f32[512,128]{1,0:T(8,128)} %get-tuple-element.5.b), custom_call_target="tpu_custom_call" | custom-call | tf_op jit(solution)/shard_map/pallas_call | solution.py:433

commit v5 on v3

--- a/solution.py
+++ b/solution.py
@@ -233,7 +233,12 @@
     def half_of(c):
         return pl.ds(pl.multiple_of(c * half, half), half)
 
-    def head_total(kind, slot, p, left_side, weight):
+    def send_midway():
+        source, there = row_s.at[:, cols(h)], mid_s.at[own_rows, :]
+        exchange_f(MID, 0, lambda t: source, there, mid_s.at[pl.ds(0, latent_count - rows_each), :])
+        mid_s[own_rows, :] = row_s[:, cols(h)]
+
+    def head_total(kind, slot, p, left_side, weight, meanwhile=None):
         give_s[p, slot] = project(left_side, weight[p, :, half_of(1 - core)]).astype(BF16)
         pair = pltpu.make_async_remote_copy(
             give_s.at[p, slot], take_s.at[p, slot], send_sem.at[p, kind + PAIRS], recv_sem.at[p, kind + PAIRS],
@@ -249,6 +254,8 @@
                 device_id=(f, lax.rem(h + d, nh)), device_id_type=MESH,
             ).start()
         outstanding.append(lambda: sent(kind, p, sum_s.at[p, slot, pl.ds(0, nh - 1)]))
+        if meanwhile is not None:
+            meanwhile()
         landed(kind, p, sum_s.at[p, slot, pl.ds(0, nh - 1)])
         halves = []
         for c in range(2):
@@ -316,7 +323,7 @@
         context = jnp.where(first, both[:rows_each], both[rows_each:]).astype(BF16)
         if p == 0:
             loaded(5, so_s)
-        rows = rows + head_total(SELF, 1, p, context, so_s)
+        rows = rows + head_total(SELF, 1, p, context, so_s, send_midway if p == 1 else None)
 
         if p == 0:
             loaded(6, mi_s)
@@ -333,9 +340,6 @@
             exchange_f(QUERY, p, lambda t: here, here, qall_s.at[p + 1, others, :])
         if p == 0:
             row_s[...] = rows
-            source, there = row_s.at[:, cols(h)], mid_s.at[own_rows, :]
-            exchange_f(MID, p, lambda t: source, there, mid_s.at[others, :])
-            mid_s[own_rows, :] = row_s[:, cols(h)]
         if p + 1 < passes:
             landed(QUERY, p, qall_s.at[p + 1, others, :])
 
@@ -346,6 +350,11 @@
     ring(0, 0, x_s.at[:, pl.ds(0, 7 * LANES)], x_s.at[:, pl.ds(0, 7 * LANES)], sib).wait_send()
     for wait in outstanding:
         wait()
+
+
+def hand_over(a, b, a_out, b_out):
+    a_out[...] = a[...]
+    b_out[...] = b[...]
 
 
 def local(nf, nh, *args):
@@ -390,7 +399,7 @@
         pltpu.SemaphoreType.DMA((passes, 12)),
         pltpu.SemaphoreType.DMA((passes, 12)),
     ]
-    return pl.pallas_call(
+    outs = pl.pallas_call(
         functools.partial(kernel, nf, nh),
         out_shape=(
             jax.ShapeDtypeStruct((rows_each, width), F32),
@@ -403,6 +412,12 @@
             collective_id=0, has_side_effects=True, vmem_limit_bytes=56 * 1024 * 1024
         ),
     )(*args)
+    return pl.pallas_call(
+        hand_over,
+        out_shape=tuple(jax.ShapeDtypeStruct(a.shape, a.dtype) for a in outs),
+        in_specs=[pl.BlockSpec(memory_space=vm)] * 2,
+        out_specs=[pl.BlockSpec(memory_space=vm)] * 2,
+    )(*outs)
 
 
 def solution(mesh):

time: 108 us -> 106 us (0.981)
  local copies, waits for them, and re-layouts: 3.14 us -> 0 us
    unnamed x2 -> x0, local copies, waits for them, and re-layouts: 3.14 us -> none
    pallas_call x0 -> x1, Pallas kernels: none -> 1.72 us  [local(): pl.pallas_call(hand_over, out_shape=tuple((jax.ShapeDtypeStruct(a.shape,...]
where the time goes in v5:
time: 106 us
  Pallas kernels  105 us (99%)
    pallas_call x1, Pallas kernels, local(): pl.pallas_call(functools.partial(kernel, nf, nh), out_shape=(jax.ShapeDty...  104 us

profile of v5, /device:TPU:1, one launch (start us, length us, event | category | flops | bytes accessed | tf_op | source)
XLA Modules:
  0.0 106.1 jit_solution(5381761097800589618)
XLA Ops:
  0.6 103.8 %shard_map.131 = (f32[16,1024]{1,0:T(8,128)}, f32[512,128]{1,0:T(8,128)}) custom-call(bf16[1024,128]{1,0:T(8,128)(2,1)} %frames.1, bf16[512,1024]{1,0:T(8,128)(2,1)} %latents.1, bf16[2,1024,128]{2,1,0:T(8,128)(2,1)} %cq.1, bf16[2,1024,128]{2,1,0:T(8,128)(2,1)} %ck.1, bf16[2,1024,128]{2,1,0:T(8,128)(2,1)} %cv.1, bf16[2,128,1024]{2,1,0:T(8,128)(2,1)} %co.1, ...), custom_call_target="tpu_custom_call" | custom-call | tf_op jit(solution)/shard_map/pallas_call | solution.py:402
  104.4 1.7 %shard_map.132 = (f32[16,1024]{1,0:T(8,128)}, f32[512,128]{1,0:T(8,128)}) custom-call(f32[16,1024]{1,0:T(8,128)} %get-tuple-element.4.a, f32[512,128]{1,0:T(8,128)} %get-tuple-element.5.b), custom_call_target="tpu_custom_call" | custom-call | tf_op jit(solution)/shard_map/pallas_call | solution.py:415

commit v6 on v5

--- a/solution.py
+++ b/solution.py
@@ -52,7 +52,7 @@
     nf, nh,
     frames, latents, cq, ck, cv, co, sq, sk, sv, so, mi, mo,
     encoded, midway,
-    x_s, lat_s, cq_s, ckv_s, co_s, sqkv_s, so_s, mi_s, mo_s,
+    x_s, xn_s, lat_s, cq_s, ckv_s, co_s, sqkv_s, so_s, mi_s, mo_s,
     k_s, vt_s, qall_s, qh_s, m_s, acc_s, o_s, st_s, po_s, ps_s, tr_s, sk_s, sv_s, give_s, take_s, sum_s, row_s, mid_s,
     w_sem, own_sem, ring_recv, ring_send, recv_sem, send_sem,
 ):
@@ -147,27 +147,21 @@
         vt_s[p, pl.ds(LANES, ONES), :] = jnp.ones((ONES, frame_count), BF16)
     loaded(2, ckv_s)
 
-    def keys_values(k):
+    def normalise(k):
         r = pl.ds(k * chunk, chunk)
-        normed = layer_norm(x_s[r, :].astype(F32)).astype(BF16)
-        both = project(normed, ckv_s[...])
-        for p in range(passes):
-            k_s[p, r, :] = both[:, 2 * p * LANES:(2 * p + 1) * LANES].astype(BF16)
-            value = both[:, (2 * p + 1) * LANES:(2 * p + 2) * LANES]
-            vt_s[p, pl.ds(0, LANES), r] = value.T.astype(BF16)
-
-    def attend_start():
-        m_s[...] = jnp.full_like(m_s, -jnp.inf)
-        acc_s[...] = jnp.zeros_like(acc_s)
-
-    def attend(p, k):
+        xn_s[r, :] = layer_norm(x_s[r, :].astype(F32)).astype(BF16)
+
+    def keys_values(p, k):
         r = pl.ds(pl.multiple_of(k * chunk, chunk), chunk)
-        scores = against(k_s[p, r, :], qh_s[...])
-        before = m_s[...]
-        highest = jnp.maximum(before, jnp.max(scores, axis=0, keepdims=True))
-        terms = jnp.exp(scores - highest).astype(BF16)
-        acc_s[...] = acc_s[...] * jnp.exp(before - highest) + project(vt_s[p, :, r], terms)
+        both = project(xn_s[r, :], ckv_s[:, pl.ds(2 * p * LANES, 2 * LANES)])
+        k_s[p, r, :] = both[:, :LANES].astype(BF16)
+        vt_s[p, pl.ds(0, LANES), r] = both[:, LANES:].T.astype(BF16)
+
+    def attend(p):
+        scores = against(k_s[p], qh_s[...])
+        highest = jnp.max(scores, axis=0, keepdims=True)
         m_s[...] = highest
+        acc_s[...] = project(vt_s[p], jnp.exp(scores - highest).astype(BF16))
 
     outstanding = []
 
@@ -211,6 +205,12 @@
         exchange_f(PART, p, lambda t: o_s.at[p, rows_of(t), :], po_s.at[p, f], parts)
         po_s[p, f] = o_s[p, own_rows, :]
         ps_s[p, f] = st_s[p, f // per_tile]
+        if p + 1 < passes:
+            def later(k, _):
+                keys_values(p + 1, k)
+                return 0
+
+            lax.fori_loop(0, CHUNKS, later, 0)
         landed(STAT, p, stats)
         levels = jnp.concatenate([ps_s[p, :, 0, :], ps_s[p, :, 1, :]], axis=0)
         tr_s[...] = levels.T
@@ -237,6 +237,12 @@
         source, there = row_s.at[:, cols(h)], mid_s.at[own_rows, :]
         exchange_f(MID, 0, lambda t: source, there, mid_s.at[pl.ds(0, latent_count - rows_each), :])
         mid_s[own_rows, :] = row_s[:, cols(h)]
+
+    midway_copy = pltpu.make_async_copy(mid_s, midway, own_sem.at[0])
+
+    def hand_midway():
+        landed(MID, 0, mid_s.at[pl.ds(0, latent_count - rows_each)])
+        midway_copy.start()
 
     def head_total(kind, slot, p, left_side, weight, meanwhile=None):
         give_s[p, slot] = project(left_side, weight[p, :, half_of(1 - core)]).astype(BF16)
@@ -265,8 +271,6 @@
             halves.append(out)
         return jnp.concatenate(halves, axis=1)
 
-    attend_start()
-
     for k in range(CHUNKS):
         kind, onward, who, to = (L, S_L, left, right) if k % 2 == 0 else (R, S_R, right, left)
         arrived(kind, k, who)
@@ -286,19 +290,13 @@
             pltpu.make_async_copy(frames.at[r, :], x_s.at[r, cols(h)], own_sem.at[k]).wait()
             for kind in (S_OWN, S_L, S_R, S_O):
                 arrived(kind, k, sib)
-            keys_values(k)
-            attend(0, k)
+            normalise(k)
+            keys_values(0, k)
 
     for p in range(passes):
         if p > 0:
-            attend_start()
             qh_s[...] = by_head(qall_s[p])
-
-            def again(k, _):
-                attend(p, k)
-                return 0
-
-            lax.fori_loop(0, CHUNKS, again, 0)
+        attend(p)
         context = attend_end(p)
         if p == 0:
             loaded(3, co_s)
@@ -308,8 +306,9 @@
             loaded(4, sqkv_s)
         self_in = layer_norm(rows).astype(BF16)
         others = pl.ds(0, latent_count - rows_each)
+        kv = project(self_in, sqkv_s[p, :, pl.ds(LANES, 2 * LANES)])
         for i, (kind, ref) in enumerate(((KEYS, sk_s), (VALUES, sv_s))):
-            ref[p, own_rows, :] = project(self_in, sqkv_s[p, :, pl.ds((i + 1) * LANES, LANES)]).astype(BF16)
+            ref[p, own_rows, :] = kv[:, i * LANES:(i + 1) * LANES].astype(BF16)
             here = ref.at[p, own_rows, :]
             exchange_f(kind, p, lambda t: here, here, ref.at[p, others, :])
         q = by_head((project(self_in, sqkv_s[p, :, pl.ds(0, LANES)]) * 0.125).astype(BF16))
@@ -331,7 +330,7 @@
         hidden = (0.5 * u * (1.0 + lax.erf(u * 0.7071067811865476))).astype(BF16)
         if p == 0:
             loaded(7, mo_s)
-        rows = rows + head_total(MLP, 2, p, hidden, mo_s)
+        rows = rows + head_total(MLP, 2, p, hidden, mo_s, hand_midway if p == 1 else None)
 
         if p + 1 < passes:
             q = (project(layer_norm(rows).astype(BF16), cq_s[p + 1]) * 0.125).astype(BF16)
@@ -344,8 +343,7 @@
             landed(QUERY, p, qall_s.at[p + 1, others, :])
 
     encoded[...] = rows
-    landed(MID, 0, mid_s.at[pl.ds(0, latent_count - rows_each)])
-    midway[...] = mid_s[...]
+    midway_copy.wait()
 
     ring(0, 0, x_s.at[:, pl.ds(0, 7 * LANES)], x_s.at[:, pl.ds(0, 7 * LANES)], sib).wait_send()
     for wait in outstanding:
@@ -365,6 +363,7 @@
     rows_each = latent_count // nf
     vm = pltpu.VMEM
     scratch = [
+        vm((frame_count, width), BF16),
         vm((frame_count, width), BF16),
         vm((latent_count, width), BF16),
         vm((passes, width, LANES), BF16),
@@ -406,7 +405,7 @@
             jax.ShapeDtypeStruct((latent_count, LANES), F32),
         ),
         in_specs=[pl.BlockSpec(memory_space=pl.ANY)] * len(args),
-        out_specs=(pl.BlockSpec(memory_space=vm), pl.BlockSpec(memory_space=vm)),
+        out_specs=(pl.BlockSpec(memory_space=vm), pl.BlockSpec(memory_space=pl.ANY)),
         scratch_shapes=scratch,
         compiler_params=pltpu.CompilerParams(
             collective_id=0, has_side_effects=True, vmem_limit_bytes=56 * 1024 * 1024

time: 106 us -> 104 us (0.981)
  Pallas kernels: 105 us -> 103 us
    pallas_call x1, Pallas kernels: 104 us -> 102 us  [local(): pl.pallas_call(functools.partial(kernel, nf, nh), out_shape=(jax.ShapeDty...]
where the time goes in v6:
time: 104 us
  Pallas kernels  103 us (99%)
    pallas_call x1, Pallas kernels, local(): pl.pallas_call(functools.partial(kernel, nf, nh), out_shape=(jax.ShapeDty...  102 us

profile of v6, /device:TPU:1, one launch (start us, length us, event | category | flops | bytes accessed | tf_op | source)
XLA Modules:
  0.0 104.1 jit_solution(11179185482867161167)
XLA Ops:
  0.6 101.8 %shard_map.131 = (f32[16,1024]{1,0:T(8,128)}, f32[512,128]{1,0:T(8,128)}) custom-call(bf16[1024,128]{1,0:T(8,128)(2,1)} %frames.1, bf16[512,1024]{1,0:T(8,128)(2,1)} %latents.1, bf16[2,1024,128]{2,1,0:T(8,128)(2,1)} %cq.1, bf16[2,1024,128]{2,1,0:T(8,128)(2,1)} %ck.1, bf16[2,1024,128]{2,1,0:T(8,128)(2,1)} %cv.1, bf16[2,128,1024]{2,1,0:T(8,128)(2,1)} %co.1, ...), custom_call_target="tpu_custom_call" | custom-call | tf_op jit(solution)/shard_map/pallas_call | solution.py:401
  102.4 1.7 %shard_map.132 = (f32[16,1024]{1,0:T(8,128)}, f32[512,128]{1,0:T(8,128)}) custom-call(f32[16,1024]{1,0:T(8,128)} %get-tuple-element.4.a, f32[512,128]{1,0:T(8,128)} %get-tuple-element.5.b), custom_call_target="tpu_custom_call" | custom-call | tf_op jit(solution)/shard_map/pallas_call | solution.py:414

commit v7 on v6

--- a/solution.py
+++ b/solution.py
@@ -245,15 +245,7 @@
         midway_copy.start()
 
     def head_total(kind, slot, p, left_side, weight, meanwhile=None):
-        give_s[p, slot] = project(left_side, weight[p, :, half_of(1 - core)]).astype(BF16)
-        pair = pltpu.make_async_remote_copy(
-            give_s.at[p, slot], take_s.at[p, slot], send_sem.at[p, kind + PAIRS], recv_sem.at[p, kind + PAIRS],
-            device_id=(f, sib), device_id_type=MESH,
-        )
-        pair.start()
-        mine = project(left_side, weight[p, :, half_of(core)])
-        pair.wait()
-        sum_s[p, slot, h] = (mine + take_s[p, slot].astype(F32)).astype(BF16)
+        sum_s[p, slot, h] = project(left_side, weight[p]).astype(BF16)
         for d in (4, 5, 3, 2, 6, 7, 1):
             pltpu.make_async_remote_copy(
                 sum_s.at[p, slot, h], sum_s.at[p, slot, h], send_sem.at[p, kind], recv_sem.at[p, kind],
@@ -263,13 +255,10 @@
         if meanwhile is not None:
             meanwhile()
         landed(kind, p, sum_s.at[p, slot, pl.ds(0, nh - 1)])
-        halves = []
-        for c in range(2):
-            out = sum_s[p, slot, c].astype(F32)
-            for i in range(c + 2, nh, 2):
-                out += sum_s[p, slot, i].astype(F32)
-            halves.append(out)
-        return jnp.concatenate(halves, axis=1)
+        out = sum_s[p, slot, 0].astype(F32)
+        for i in range(1, nh):
+            out += sum_s[p, slot, i].astype(F32)
+        return out
 
     for k in range(CHUNKS):
         kind, onward, who, to = (L, S_L, left, right) if k % 2 == 0 else (R, S_R, right, left)
@@ -388,7 +377,7 @@
         vm((passes, latent_count, LANES), BF16),
         vm((passes, 3, rows_each, width // 2), BF16),
         vm((passes, 3, rows_each, width // 2), BF16),
-        vm((passes, 3, nh, rows_each, width // 2), BF16),
+        vm((passes, 3, nh, rows_each, width), BF16),
         vm((rows_each, width), F32),
         vm((latent_count, LANES), F32),
         pltpu.SemaphoreType.DMA((8,)),

time: 104 us -> 101 us (0.971)
  Pallas kernels: 103 us -> 101 us
    pallas_call x1, Pallas kernels: 102 us -> 99 us  [local(): pl.pallas_call(functools.partial(kernel, nf, nh), out_shape=(jax.ShapeDty...]
where the time goes in v7:
time: 101 us
  Pallas kernels  101 us (100%)
    pallas_call x1, Pallas kernels, local(): pl.pallas_call(functools.partial(kernel, nf, nh), out_shape=(jax.ShapeDty...  99 us

profile of v7, /device:TPU:1, one launch (start us, length us, event | category | flops | bytes accessed | tf_op | source)
XLA Modules:
  0.0 101.4 jit_solution(2920593250042833402)
XLA Ops:
  0.6 99.0 %shard_map.131 = (f32[16,1024]{1,0:T(8,128)}, f32[512,128]{1,0:T(8,128)}) custom-call(bf16[1024,128]{1,0:T(8,128)(2,1)} %frames.1, bf16[512,1024]{1,0:T(8,128)(2,1)} %latents.1, bf16[2,1024,128]{2,1,0:T(8,128)(2,1)} %cq.1, bf16[2,1024,128]{2,1,0:T(8,128)(2,1)} %ck.1, bf16[2,1024,128]{2,1,0:T(8,128)(2,1)} %cv.1, bf16[2,128,1024]{2,1,0:T(8,128)(2,1)} %co.1, ...), custom_call_target="tpu_custom_call" | custom-call | tf_op jit(solution)/shard_map/pallas_call | solution.py:390
  99.7 1.7 %shard_map.132 = (f32[16,1024]{1,0:T(8,128)}, f32[512,128]{1,0:T(8,128)}) custom-call(f32[16,1024]{1,0:T(8,128)} %get-tuple-element.4.a, f32[512,128]{1,0:T(8,128)} %get-tuple-element.5.b), custom_call_target="tpu_custom_call" | custom-call | tf_op jit(solution)/shard_map/pallas_call | solution.py:403

commit v8 on v7

--- a/solution.py
+++ b/solution.py
@@ -185,23 +185,23 @@
 
     def attend_end(p):
         total = acc_s[pl.ds(LANES, 1), :]
+        level = m_s[...] + jnp.log(total)
+        for t in range(latent_count // LANES):
+            for i in range(2):
+                at = i * latent_count + t * LANES
+                st_s[p, t, pl.ds(i, 1), :] = level[:, at:at + LANES]
+
+        def rows_of(t):
+            return pl.ds(pl.multiple_of(t * rows_each, rows_each), rows_each)
+
+        per_tile = LANES // rows_each
+        stats, parts = ps_s.at[p, pl.ds(0, nf - 1)], po_s.at[p, pl.ds(0, nf - 1)]
+        exchange_f(STAT, p, lambda t: st_s.at[p, t // per_tile], ps_s.at[p, f], stats)
         value = acc_s[pl.ds(0, LANES), :] / total
         both = jnp.concatenate(
             [value[:HEAD_DIM, :latent_count], value[HEAD_DIM:, latent_count:]], axis=0
         )
         o_s[p] = both.T.astype(BF16)
-        level = m_s[...] + jnp.log(total)
-        for t in range(latent_count // LANES):
-            for i in range(2):
-                at = i * latent_count + t * LANES
-                st_s[p, t, pl.ds(i, 1), :] = level[:, at:at + LANES]
-
-        def rows_of(t):
-            return pl.ds(pl.multiple_of(t * rows_each, rows_each), rows_each)
-
-        per_tile = LANES // rows_each
-        stats, parts = ps_s.at[p, pl.ds(0, nf - 1)], po_s.at[p, pl.ds(0, nf - 1)]
-        exchange_f(STAT, p, lambda t: st_s.at[p, t // per_tile], ps_s.at[p, f], stats)
         exchange_f(PART, p, lambda t: o_s.at[p, rows_of(t), :], po_s.at[p, f], parts)
         po_s[p, f] = o_s[p, own_rows, :]
         ps_s[p, f] = st_s[p, f // per_tile]

time: 101 us -> 101 us (level)
  no operation moved by 1% of the time
where the time goes in v8:
time: 101 us
  Pallas kernels  101 us (100%)
    pallas_call x1, Pallas kernels, local(): pl.pallas_call(functools.partial(kernel, nf, nh), out_shape=(jax.ShapeDty...  98.8 us

profile of v8, /device:TPU:1, one launch (start us, length us, event | category | flops | bytes accessed | tf_op | source)
XLA Modules:
  0.0 101.2 jit_solution(14633146416445972583)
XLA Ops:
  0.6 98.8 %shard_map.131 = (f32[16,1024]{1,0:T(8,128)}, f32[512,128]{1,0:T(8,128)}) custom-call(bf16[1024,128]{1,0:T(8,128)(2,1)} %frames.1, bf16[512,1024]{1,0:T(8,128)(2,1)} %latents.1, bf16[2,1024,128]{2,1,0:T(8,128)(2,1)} %cq.1, bf16[2,1024,128]{2,1,0:T(8,128)(2,1)} %ck.1, bf16[2,1024,128]{2,1,0:T(8,128)(2,1)} %cv.1, bf16[2,128,1024]{2,1,0:T(8,128)(2,1)} %co.1, ...), custom_call_target="tpu_custom_call" | custom-call | tf_op jit(solution)/shard_map/pallas_call | solution.py:390
  99.4 1.7 %shard_map.132 = (f32[16,1024]{1,0:T(8,128)}, f32[512,128]{1,0:T(8,128)}) custom-call(f32[16,1024]{1,0:T(8,128)} %get-tuple-element.4.a, f32[512,128]{1,0:T(8,128)} %get-tuple-element.5.b), custom_call_target="tpu_custom_call" | custom-call | tf_op jit(solution)/shard_map/pallas_call | solution.py:403
